TPU v7x, 32 devices: a whole 2x2x4 slice. The times are simulated.
32 devices in a mesh: grid: 8 (over z, x), help: 4 (over y, core).
Axes of the slice: x: 2, y: 2, z: 4, core: 2. Of those that a mesh axis runs over, the one named last changes fastest.
Arguments:
- corners: float32 [24, 65536], P(None, 'grid'), as said below
- solution: float32 [40, 65536], P(None, 'grid'), may hold values from -6 to 6
- loc_xyz: float32 [3, 262144], P(None, ('grid', 'help')), as said below
- loc_cell: int32 [262144], P(('grid', 'help')), may hold values from 0 to 8191, as said below
- loc_live: int32 [8, 4], P('grid', 'help'), may hold values from 1 to 8192, 16384 in all within a row
- rem_xyz: float32 [3, 1024], P(None, ('grid', 'help')), as said below
- rem_cell: int32 [1024], P(('grid', 'help')), may hold values from 0 to 8191, as said below
- rem_count: int32 [32, 8], P(('grid', 'help')), may hold values from 1 to 4
Outputs:
- loc_values: float32 [5, 262144], P(None, ('grid', 'help'))
- rem_values: float32 [5, 1024], P(None, ('grid', 'help'))
Inputs may be any that keep to these rules, and one draw needn't show every extreme that they name: `corners`: each cell's corner k lies within a quarter of the cell's half edge of the corner with signs s_k of an axis-aligned cube. `loc_xyz`: each receptor is the image under its donor cell's trilinear map of a point in the cube of half edge 0.9. `rem_xyz`: each receptor is the image under its donor cell's trilinear map of a point in the cube of half edge 0.9. `loc_cell`: a cell of the owner's partition. `rem_cell`: a cell of the partition named by the slot. `loc_live`: live slots are those of lowest rank on each device; in each help group one device has 8192 live slots and the group has 16384 in all. `rem_count`: live slots of a partition come first.
All inputs are finite; a program needn't handle non-finite values.
Results may differ from a plain program's by a relative error of at most 0.0003.
Values sent between devices are 32-bit elements; how exact they have to be, the bound alone decides.
No kernel may reach another device: no remote copies, remote signals or barrier semaphores. Data moves between devices by JAX's collectives and lax.ppermute only.
A program may use at most 64 MiB of HBM per device.

v0:
```python
import jax
import jax.numpy as jnp
from jax import lax
from jax.sharding import PartitionSpec as P

PASSES = 3


def solve_three(jacobian, residual):
    row_zero, row_one, row_two = jacobian
    cof_00 = row_one[1] * row_two[2] - row_one[2] * row_two[1]
    cof_01 = row_one[2] * row_two[0] - row_one[0] * row_two[2]
    cof_02 = row_one[0] * row_two[1] - row_one[1] * row_two[0]
    cof_10 = row_zero[2] * row_two[1] - row_zero[1] * row_two[2]
    cof_11 = row_zero[0] * row_two[2] - row_zero[2] * row_two[0]
    cof_12 = row_zero[1] * row_two[0] - row_zero[0] * row_two[1]
    cof_20 = row_zero[1] * row_one[2] - row_zero[2] * row_one[1]
    cof_21 = row_zero[2] * row_one[0] - row_zero[0] * row_one[2]
    cof_22 = row_zero[0] * row_one[1] - row_zero[1] * row_one[0]
    determinant = row_zero[0] * cof_00 + row_zero[1] * cof_01 + row_zero[2] * cof_02
    step_x = (cof_00 * residual[0] + cof_10 * residual[1] + cof_20 * residual[2]) / determinant
    step_y = (cof_01 * residual[0] + cof_11 * residual[1] + cof_21 * residual[2]) / determinant
    step_z = (cof_02 * residual[0] + cof_12 * residual[1] + cof_22 * residual[2]) / determinant
    return [step_x, step_y, step_z]


def corner_weights(local_xi):
    lower_half = [(1.0 - value) * 0.5 for value in local_xi]
    upper_half = [(1.0 + value) * 0.5 for value in local_xi]
    factors_all = []
    slopes_all = []
    for corner in range(8):
        factors = [
            upper_half[dim_idx] if corner >> dim_idx & 1 else lower_half[dim_idx]
            for dim_idx in range(3)
        ]
        slopes = [0.5 if corner >> dim_idx & 1 else -0.5 for dim_idx in range(3)]
        factors_all.append(factors)
        slopes_all.append(slopes)
    return (factors_all, slopes_all)


def interpolate(points, blocks, fields):
    local_xi = [jnp.zeros_like(points[0]) for dim_idx in range(3)]
    for newton_pass in range(PASSES):
        factors_all, slopes_all = corner_weights(local_xi)
        residual = [-points[dim_idx] for dim_idx in range(3)]
        jacobian = [[jnp.zeros_like(points[0]) for col_idx in range(3)] for row_idx in range(3)]
        for corner in range(8):
            factors = factors_all[corner]
            slopes = slopes_all[corner]
            weight = factors[0] * factors[1] * factors[2]
            partials = [
                slopes[0] * factors[1] * factors[2],
                factors[0] * slopes[1] * factors[2],
                factors[0] * factors[1] * slopes[2],
            ]
            for row_idx in range(3):
                corner_coord = blocks[8 * row_idx + corner]
                residual[row_idx] = residual[row_idx] + weight * corner_coord
                for col_idx in range(3):
                    jacobian[row_idx][col_idx] = (
                        jacobian[row_idx][col_idx] + partials[col_idx] * corner_coord
                    )
        newton_step = solve_three(jacobian, residual)
        local_xi = [local_xi[dim_idx] - newton_step[dim_idx] for dim_idx in range(3)]
    factors_all, slopes_all = corner_weights(local_xi)
    outputs = []
    for field_idx in range(5):
        total_value = jnp.zeros_like(points[0])
        for corner in range(8):
            factors = factors_all[corner]
            weight = factors[0] * factors[1] * factors[2]
            total_value = total_value + weight * fields[8 * field_idx + corner]
        outputs.append(total_value)
    return jnp.stack(outputs, 0)


def at_cells(points, cell_index, corners, solution):
    return interpolate(
        points, jnp.take(corners, cell_index, axis=1), jnp.take(solution, cell_index, axis=1)
    )


def per_device(corners, solution, loc_xyz, loc_cell, loc_live, rem_xyz, rem_cell, rem_count):
    grid_count = lax.axis_size("grid")
    slot_depth = rem_cell.shape[0] // grid_count
    wanted = rem_cell.reshape(slot_depth, grid_count)
    remote_live = (
        lax.broadcasted_iota(jnp.int32, (slot_depth, grid_count), 0) < rem_count
    ).reshape(-1)
    asked = lax.all_to_all(wanted, "grid", split_axis=1, concat_axis=1, tiled=True)
    corner_blocks = jnp.take(corners, asked, axis=1)
    field_blocks = jnp.take(solution, asked, axis=1)
    corner_blocks, field_blocks = (
        lax.all_to_all(corner_blocks, "grid", split_axis=2, concat_axis=2, tiled=True),
        lax.all_to_all(field_blocks, "grid", split_axis=2, concat_axis=2, tiled=True),
    )
    remote_results = interpolate(
        rem_xyz, corner_blocks.reshape(24, -1), field_blocks.reshape(40, -1)
    )
    rem_values = jnp.where(remote_live[None, :], remote_results, 0.0)
    loc_dev = loc_cell.shape[0]
    live_count = loc_live.reshape(())
    help_count = lax.axis_size("help")
    slab = loc_dev // help_count
    helper = lax.axis_index("help")
    stacked = jnp.concatenate([loc_xyz, loc_cell.astype(jnp.float32)[None, :]], 0)
    dealt = stacked.reshape(4, help_count, slab)
    count_rows = jnp.full((1, help_count, 1), live_count.astype(jnp.float32))
    arrived, arrived_counts = (
        lax.all_to_all(dealt, "help", split_axis=1, concat_axis=1, tiled=True),
        lax.all_to_all(count_rows, "help", split_axis=1, concat_axis=1, tiled=True),
    )
    source_counts = arrived_counts[0, :, 0].astype(jnp.int32)
    per_source = jnp.maximum(source_counts - helper + help_count - 1, 0) // help_count
    end_marks = jnp.cumsum(per_source)
    start_marks = end_marks - per_source
    bal_rows = (2 * loc_dev // help_count + help_count + 127) // 128 * 128
    position = jnp.arange(bal_rows, dtype=jnp.int32)
    source_idx = jnp.sum((position[:, None] >= end_marks[None, :]).astype(jnp.int32), axis=1)
    is_valid = position < end_marks[-1]
    source_idx = jnp.minimum(source_idx, help_count - 1)
    one_hot = source_idx[:, None] == jnp.arange(help_count, dtype=jnp.int32)[None, :]
    source_start = jnp.sum(jnp.where(one_hot, start_marks[None, :], 0), axis=1)
    flat_index = jnp.where(is_valid, source_idx * slab + position - source_start, 0)
    received_rows = arrived.reshape(4, help_count * slab)
    picked = jnp.take(received_rows, flat_index, axis=1)
    picked_cells = picked[3].astype(jnp.int32)
    results = at_cells(picked[:3], picked_cells, corners, solution)
    results = jnp.where(is_valid[None, :], results, 0.0)
    slab_pos = jnp.arange(slab, dtype=jnp.int32)
    in_range = slab_pos[None, :] < per_source[:, None]
    back_index = jnp.where(in_range, start_marks[:, None] + slab_pos[None, :], 0)
    handed = jnp.take(results, back_index.reshape(-1), axis=1).reshape(5, help_count, slab)
    handed = jnp.where(in_range[None, :, :], handed, 0.0)
    returned = lax.all_to_all(handed, "help", split_axis=1, concat_axis=1, tiled=True)
    loc_values = returned.reshape(5, loc_dev)
    return (loc_values, rem_values)


def solution(mesh):
    placed = (
        P(None, "grid"),
        P(None, "grid"),
        P(None, ("grid", "help")),
        P(("grid", "help")),
        P("grid", "help"),
        P(None, ("grid", "help")),
        P(("grid", "help")),
        P(("grid", "help"), None),
    )
    return jax.shard_map(
        per_device,
        mesh=mesh,
        in_specs=placed,
        out_specs=(P(None, ("grid", "help")), P(None, ("grid", "help"))),
        check_vma=False,
    )
```

profile of v0, /device:TPU:0, one launch (start us, length us, event | category | flops | bytes accessed | tf_op | source)
XLA Modules:
  0.0 153.6 jit_solution(14517777080711947607)
XLA Ops:
  1.9 4.2 %all-to-all-start = ((f32[1,4,1]{2,0,1:T(1,128)}), f32[1,4,1]{2,0,1:T(1,128)S(1)}, u32[]{:S(2)}, u32[]{:S(2)}) async-start(f32[1,4,1]{2,0,1:T(1,128)} %broadcast_in_dim.135), calls=%async_computation | async-start | bytes 4096 | tf_op jit(solution)/shard_map/all_to_all | solution.py:113
  7.4 0.7 all_to_all.24
  8.8 0.8 convert_element_type.55
  9.6 1.0 concatenate.8
  10.7 0.7 copy.519
  11.4 3.7 %copy.522 = f32[24,8192]{0,1:T(8,128)} copy(f32[24,8192]{1,0:T(8,128)} %param.8) | data formatting | bytes 1572864 | tf_op args[0]
  15.1 2.7 %copy.524 = f32[40,8192]{0,1:T(8,128)} copy(f32[40,8192]{1,0:T(8,128)S(1)} %copy-done) | data formatting | bytes 2621440 | tf_op args[1]
  17.8 6.3 %all-to-all-start.3 = ((s32[4,8,1]{0,2,1:T(1,128)}), s32[4,8,1]{0,2,1:T(1,128)S(1)}, u32[]{:S(2)}, u32[]{:S(2)}) async-start(s32[4,8,1]{0,2,1:T(1,128)} %copy.528), calls=%async_computation.3 | async-start | bytes 8192 | tf_op jit(solution)/shard_map/all_to_all | solution.py:92
  26.4 1.2 iota_compare_fusion.3
  28.2 2.3 %all-to-all-done.3 = s32[4,8,1]{0,2,1:T(1,128)S(1)} async-done(((s32[4,8,1]{0,2,1:T(1,128)}), s32[4,8,1]{0,2,1:T(1,128)S(1)}, u32[]{:S(2)}, u32[]{:S(2)}) %all-to-all-start.3) | async-done | bytes 160 | tf_op jit(solution)/shard_map/all_to_all | solution.py:92
  30.9 2.8 %gather_fusion.4 = f32[32,24]{1,0:T(8,128)S(1)} fusion(f32[24,8192]{0,1:T(8,128)} %copy.522, s32[1024]{0:T(1024)S(1)} %pad_clamp_fusion.2), kind=kCustom, calls=%fused_computation.4 | custom fusion | bytes 6272 | tf_op jit(solution)/shard_map/jit(_take)/gather | solution.py:93
  34.3 3.7 %all-to-all-start.4 = ((f32[24,4,8]{0,1,2:T(4,128)}), f32[24,4,8]{0,1,2:T(4,128)S(1)}, u32[]{:S(2)}, u32[]{:S(2)}) async-start(f32[24,4,8]{0,1,2:T(4,128)} %fusion.39), calls=%async_computation.4 | async-start | bytes 32768 | tf_op jit(solution)/shard_map/all_to_all | solution.py:96
  38.1 2.8 %gather_fusion.5 = f32[32,40]{1,0:T(8,128)S(1)} fusion(f32[40,8192]{0,1:T(8,128)} %copy.524, s32[1024]{0:T(1024)S(1)} %pad_clamp_fusion.2), kind=kCustom, calls=%fused_computation.5 | custom fusion | bytes 10368 | tf_op jit(solution)/shard_map/jit(_take)/gather | solution.py:94
  41.6 3.0 %all-to-all-done.4 = f32[24,4,8]{0,1,2:T(4,128)S(1)} async-done(((f32[24,4,8]{0,1,2:T(4,128)}), f32[24,4,8]{0,1,2:T(4,128)S(1)}, u32[]{:S(2)}, u32[]{:S(2)}) %all-to-all-start.4) | async-done | bytes 3104 | tf_op jit(solution)/shard_map/all_to_all | solution.py:96
  44.6 3.3 %all-to-all-start.5 = ((f32[8,1,160]{2,1,0:T(1,128)}), f32[8,1,160]{2,1,0:T(1,128)S(1)}, u32[]{:S(2)}, u32[]{:S(2)}) async-start(f32[8,1,160]{2,1,0:T(1,128)} %reshape.2072), calls=%async_computation.5 | async-start | bytes 16384 | tf_op jit(solution)/shard_map/all_to_all | solution.py:97
  53.1 1.2 all-to-all-done.5
  54.3 3.5 %all-to-all-start.1 = ((f32[4,4,2048]{2,0,1:T(4,128)}), f32[4,4,2048]{2,0,1:T(4,128)S(1)}, u32[]{:S(2)}, u32[]{:S(2)}) async-start(f32[4,4,2048]{2,0,1:T(4,128)} %copy.519), calls=%async_computation.1 | async-start | bytes 262144 | tf_op jit(solution)/shard_map/all_to_all | solution.py:112
  67.5 2.7 %copy.520 = f32[4,4,2048]{0,2,1:T(8,128)} copy(f32[4,4,2048]{2,0,1:T(4,128)S(1)} %all-to-all-done.1) | data formatting | bytes 262144 | tf_op jit(solution)/shard_map/all_to_all | solution.py:112
  70.2 9.3 %gather_fusion = f32[4224,4]{1,0:T(8,128)S(1)} fusion(f32[4,8192]{0,1:T(8,128)} %bitcast.45, s32[5120]{0:T(1024)S(1)} %pad_clamp_fusion.1), kind=kCustom, calls=%fused_computation | custom fusion | bytes 152064 | tf_op jit(solution)/shard_map/jit(_take)/gather | solution.py:128
  80.4 10.9 %gather_fusion.1 = f32[4224,24]{1,0:T(8,128)} fusion(f32[24,8192]{0,1:T(8,128)} %copy.522, s32[5120]{0:T(1024)S(1)} %pad_clamp_fusion), kind=kCustom, calls=%fused_computation.1 | custom fusion | bytes 827904 | tf_op jit(solution)/shard_map/jit(_take)/gather | solution.py:81
  91.3 9.3 %gather_fusion.2 = f32[4224,40]{1,0:T(8,128)S(1)} fusion(f32[40,8192]{0,1:T(8,128)} %copy.524, s32[5120]{0:T(1024)S(1)} %pad_clamp_fusion), kind=kCustom, calls=%fused_computation.2 | custom fusion | bytes 1368576 | tf_op jit(solution)/shard_map/jit(_take)/gather | solution.py:81
  100.7 2.2 %copy.523 = f32[4224,24]{0,1:T(8,128)S(1)} copy(f32[4224,24]{1,0:T(8,128)} %gather_fusion.1) | data formatting | bytes 811008 | tf_op jit(solution)/shard_map/jit(_take)/gather | solution.py:81
  102.9 1.7 %multiply_multiply_fusion.30 = (f32[1,4224]{1,0:T(1,128)S(1)}, f32[1,4224]{1,0:T(1,128)S(1)}, f32[1,4224]{1,0:T(1,128)S(1)}, f32[1,4224]{1,0:T(1,128)S(1)}, f32[...) fusion(f32[24,4224]{1,0:T(8,128)S(1)} %select_bitcast_fusion.1,, ...), kind=kLoop, calls=%fused_computation.223 | loop fusion | flops 743424 | bytes 709632 | tf_op jit(solution)/shard_map/mul | solution.py:56
  105.2 0.8 select_bitcast_fusion
  106.0 2.5 %multiply_multiply_fusion.11 = (f32[1,4224]{1,0:T(1,128)S(1)}, f32[1,4224]{1,0:T(1,128)S(1)}, f32[1,4224]{1,0:T(1,128)S(1)}, f32[1,4224]{1,0:T(1,128)S(1)}, f32[...) fusion(f32[1,4224]{1,0:T(1,128)S(1)} %get-tuple-element.100, ...), kind=kLoop, calls=%fused_computation.204 | loop fusion | flops 1313664 | bytes 1013760 | tf_op jit(solution)/shard_map/mul | solution.py:56
  108.6 1.6 %fusion.42 = (f32[1,4224]{1,0:T(1,128)S(1)}, f32[1,4224]{1,0:T(1,128)S(1)}, f32[1,4224]{1,0:T(1,128)S(1)}, f32[1,4224]{1,0:T(1,128)S(1)}, f32[1,4224]{1,0:T(1,12...) fusion(f32[1,4224]{1,0:T(1,128)S(1)} %get-tuple-element.84, ...), kind=kLoop, calls=%fused_computation.277 | loop fusion | flops 1296768 | bytes 1047552 | tf_op jit(solution)/shard_map/mul | solution.py:73
  112.0 27.8 %gather_fusion.3 = f32[8192,5]{1,0:T(8,128)} fusion(f32[5,4224]{0,1:T(8,128)S(1)} %copy.526, s32[8192]{0:T(1024)S(1)} %broadcast_clamp_fusion), kind=kCustom, calls=%fused_computation.3 | custom fusion | bytes 360448 | tf_op jit(solution)/shard_map/jit(_take)/gather | solution.py:135
  139.8 2.9 %copy.527 = f32[5,4,2048]{2,0,1:T(8,128)S(1)} copy(f32[5,4,2048]{0,2,1:T(8,128)} %bitcast.46) | data formatting | bytes 327680 | tf_op jit(solution)/shard_map/jit(_take)/gather | solution.py:135
  142.7 0.8 select_select_fusion
  143.5 3.4 %all-to-all-start.2 = ((f32[5,4,2048]{2,0,1:T(8,128)}), f32[5,4,2048]{2,0,1:T(8,128)S(1)}, u32[]{:S(2)}, u32[]{:S(2)}) async-start(f32[5,4,2048]{2,0,1:T(8,128)} %select_select_fusion), calls=%async_computation.2 | async-start | bytes 524288 | tf_op jit(solution)/shard_map/all_to_all | solution.py:137
  147.5 5.4 %all-to-all-done.2 = f32[5,4,2048]{2,0,1:T(8,128)S(1)} async-done(((f32[5,4,2048]{2,0,1:T(8,128)}), f32[5,4,2048]{2,0,1:T(8,128)S(1)}, u32[]{:S(2)}, u32[]{:S(2)}) %all-to-all-start.2) | async-done | bytes 163872 | tf_op jit(solution)/shard_map/all_to_all | solution.py:137
  152.9 0.7 copy.612
  (214 shorter events, 26.1 us)
Async XLA Ops:
  1.9 15.9 %all-to-all-start = ((f32[1,4,1]{2,0,1:T(1,128)}), f32[1,4,1]{2,0,1:T(1,128)S(1)}, u32[]{:S(2)}, u32[]{:S(2)}) async-start(f32[1,4,1]{2,0,1:T(1,128)} %broadcast_in_dim.135), calls=%async_computation | async-start | bytes 4096 | tf_op jit(solution)/shard_map/all_to_all | solution.py:113
  11.4 3.7 %copy-start = (f32[40,8192]{1,0:T(8,128)S(1)}, f32[40,8192]{1,0:T(8,128)}, u32[]{:S(2)}) copy-start(f32[40,8192]{1,0:T(8,128)} %param.9) | copy-start | bytes 3932164
  17.8 35.0 %copy-start.5 = (f32[3,32]{1,0:T(4,128)S(1)}, f32[3,32]{1,0:T(4,128)}, u32[]{:S(2)}) copy-start(f32[3,32]{1,0:T(4,128)} %param.13) | copy-start | bytes 1156
  17.8 12.7 %all-to-all-start.3 = ((s32[4,8,1]{0,2,1:T(1,128)}), s32[4,8,1]{0,2,1:T(1,128)S(1)}, u32[]{:S(2)}, u32[]{:S(2)}) async-start(s32[4,8,1]{0,2,1:T(1,128)} %copy.528), calls=%async_computation.3 | async-start | bytes 8192 | tf_op jit(solution)/shard_map/all_to_all | solution.py:92
  34.3 10.3 %all-to-all-start.4 = ((f32[24,4,8]{0,1,2:T(4,128)}), f32[24,4,8]{0,1,2:T(4,128)S(1)}, u32[]{:S(2)}, u32[]{:S(2)}) async-start(f32[24,4,8]{0,1,2:T(4,128)} %fusion.39), calls=%async_computation.4 | async-start | bytes 32768 | tf_op jit(solution)/shard_map/all_to_all | solution.py:96
  44.6 9.7 %all-to-all-start.5 = ((f32[8,1,160]{2,1,0:T(1,128)}), f32[8,1,160]{2,1,0:T(1,128)S(1)}, u32[]{:S(2)}, u32[]{:S(2)}) async-start(f32[8,1,160]{2,1,0:T(1,128)} %reshape.2072), calls=%async_computation.5 | async-start | bytes 16384 | tf_op jit(solution)/shard_map/all_to_all | solution.py:97
  54.3 13.2 %all-to-all-start.1 = ((f32[4,4,2048]{2,0,1:T(4,128)}), f32[4,4,2048]{2,0,1:T(4,128)S(1)}, u32[]{:S(2)}, u32[]{:S(2)}) async-start(f32[4,4,2048]{2,0,1:T(4,128)} %copy.519), calls=%async_computation.1 | async-start | bytes 262144 | tf_op jit(solution)/shard_map/all_to_all | solution.py:112
  100.6 2.2 %copy-start.1 = (pred[4224]{0:T(1024)(128)(4,1)}, pred[4224]{0:T(1024)(128)(4,1)S(1)}, u32[]{:S(2)}) copy-start(pred[4224]{0:T(1024)(128)(4,1)S(1)} %compare_and_fusion.1) | copy-start | bytes 12676
  106.0 5.2 %copy-start.4 = (pred[4224]{0:T(1024)(128)(4,1)S(1)}, pred[4224]{0:T(1024)(128)(4,1)}, u32[]{:S(2)}) copy-start(pred[4224]{0:T(1024)(128)(4,1)} %get-tuple-element.199) | copy-start | bytes 12676
  139.8 2.9 %copy-start.2 = (pred[4,2048]{1,0:T(4,128)(4,1)S(1)}, pred[4,2048]{1,0:T(4,128)(4,1)}, u32[]{:S(2)}) copy-start(pred[4,2048]{1,0:T(4,128)(4,1)} %get-tuple-element.197) | copy-start | bytes 24580
  139.8 2.9 %copy-start.3 = (pred[4,2048]{1,0:T(4,128)(4,1)S(1)}, pred[4,2048]{1,0:T(4,128)(4,1)}, u32[]{:S(2)}) copy-start(pred[4,2048]{1,0:T(4,128)(4,1)} %get-tuple-element.198) | copy-start | bytes 24580
  139.8 7.1 %copy-start.6 = (pred[32]{0:T(512)(128)(4,1)S(1)}, pred[32]{0:T(512)(128)(4,1)}, u32[]{:S(2)}) copy-start(pred[32]{0:T(512)(128)(4,1)} %lt.158) | copy-start | bytes 100
  143.5 9.4 %all-to-all-start.2 = ((f32[5,4,2048]{2,0,1:T(8,128)}), f32[5,4,2048]{2,0,1:T(8,128)S(1)}, u32[]{:S(2)}, u32[]{:S(2)}) async-start(f32[5,4,2048]{2,0,1:T(8,128)} %select_select_fusion), calls=%async_computation.2 | async-start | bytes 524288 | tf_op jit(solution)/shard_map/all_to_all | solution.py:137
where the time goes:
time: 155 us; the launch traced here: 154 us
  local copies, waits for them, and re-layouts  99.6 us (64%)
  starting transfers between devices  24.4 us (16%)
  other arithmetic  15.9 us (10%)
  waiting for transfers between devices  12 us (8%)
  between operations  1.71 us (1%)
    gather x2, local copies, waits for them, and re-layouts, per_device(): jnp.take(results, back_index.reshape(-1), axis=1)  30.7 us
    gather x2, local copies, waits for them, and re-layouts, at_cells(): jnp.take(corners, cell_index, axis=1)  13.1 us
    gather x2, local copies, waits for them, and re-layouts, per_device(): picked = jnp.take(received_rows, flat_index, axis=1)  9.97 us
    gather x2, local copies, waits for them, and re-layouts, at_cells(): jnp.take(solution, cell_index, axis=1)  9.93 us
    unnamed x20, local copies, waits for them, and re-layouts  7.91 us
    all_to_all x1, starting transfers between devices, per_device(): lax.all_to_all(wanted, 'grid', split_axis=1, concat_axis=1, tiled=True)  6.32 us
    all_to_all x1, waiting for transfers between devices, per_device(): lax.all_to_all(handed, 'help', split_axis=1, concat_axis=1, tiled=True)  5.39 us
    slice x43, local copies, waits for them, and re-layouts, interpolate(): total_value = total_value + weight * fields[8 * field_idx + corner]  4.64 us
  transfers between devices with their start and end apart: 6, of which 4 were waited for; matrix products, arithmetic and copies ran while one was open for 22% of the time, Pallas kernels for 0%

commit v1 on v0

v1 whole, which is shorter than its diff:
```python
import functools
import jax
import jax.numpy as jnp
from jax import lax
from jax.experimental import pallas as pl
from jax.experimental.pallas import tpu as pltpu
from jax.sharding import PartitionSpec as P

PASSES = 3
LANES = 128
GROUP = 8 * LANES
ROWS = 64
VMEM_BYTES = 48 << 20


def monomials(corner):
    values = list(corner)
    for bit in (1, 2, 4):
        fresh = list(values)
        for k in range(8):
            if not k & bit:
                fresh[k] = values[k] + values[k | bit]
                fresh[k | bit] = values[k | bit] - values[k]
        values = fresh
    return values


def newton_step(jac, res):
    (a0, a1, a2), (b0, b1, b2), (c0, c1, c2) = jac
    k00 = b1 * c2 - b2 * c1
    k01 = b2 * c0 - b0 * c2
    k02 = b0 * c1 - b1 * c0
    k10 = a2 * c1 - a1 * c2
    k11 = a0 * c2 - a2 * c0
    k12 = a1 * c0 - a0 * c1
    k20 = a1 * b2 - a2 * b1
    k21 = a2 * b0 - a0 * b2
    k22 = a0 * b1 - a1 * b0
    inverse = 1.0 / (a0 * k00 + a1 * k01 + a2 * k02)
    return (
        (k00 * res[0] + k10 * res[1] + k20 * res[2]) * inverse,
        (k01 * res[0] + k11 * res[1] + k21 * res[2]) * inverse,
        (k02 * res[0] + k12 * res[1] + k22 * res[2]) * inverse,
    )


def interpolate(points, value):
    coefs = [monomials([value(8 * i + k) for k in range(8)]) for i in range(3)]
    step = newton_step(
        [[c[1], c[2], c[4]] for c in coefs], [coefs[i][0] - points[i] for i in range(3)]
    )
    xi = [-s for s in step]
    for _ in range(PASSES - 1):
        x, y, z = xi
        jac, res = [], []
        for i in range(3):
            c = coefs[i]
            a0 = c[0] + c[4] * z
            a1 = c[1] + c[5] * z
            a2 = c[2] + c[6] * z
            a3 = c[3] + c[7] * z
            dx = a1 + a3 * y
            dy = a2 + a3 * x
            dz = (c[4] + c[6] * y) + (c[5] + c[7] * y) * x
            jac.append([dx, dy, dz])
            res.append((a0 + a2 * y) + dx * x - points[i])
        step = newton_step(jac, res)
        xi = [xi[d] - step[d] for d in range(3)]
    low = [0.5 - 0.5 * v for v in xi]
    high = [0.5 + 0.5 * v for v in xi]
    plane = [p * q for q in (low[1], high[1]) for p in (low[0], high[0])]
    weights = [w * q for q in (low[2], high[2]) for w in plane]
    outs = []
    for f in range(5):
        total = weights[0] * value(24 + 8 * f)
        for k in range(1, 8):
            total = total + weights[k] * value(24 + 8 * f + k)
        outs.append(total)
    return outs


def request_kernel(xyz_ref, cell_ref, count_ref, out_ref):
    grid, depth, _ = out_ref.shape
    slots = xyz_ref.shape[1]
    width = -(-slots // LANES) * LANES
    wide = lambda a: a if a.shape[1] == width else jnp.pad(a, ((0, 0), (0, width - a.shape[1])))
    stack = jnp.concatenate(
        [
            jnp.zeros((ROWS, width), jnp.float32),
            wide(xyz_ref[...]),
            wide(cell_ref[...].astype(jnp.float32)),
            wide(count_ref[...].astype(jnp.float32)),
            jnp.zeros((LANES - ROWS - 5, width), jnp.float32),
        ],
        0,
    )
    turned = jnp.concatenate(
        [stack[:, k : k + LANES].T for k in range(0, width, LANES)], 0
    )
    counts = turned[0:grid, ROWS + 4 : ROWS + 5]
    lane = lax.broadcasted_iota(jnp.int32, (grid, LANES), 1)
    for c in range(depth):
        live = jnp.where(counts > float(c), 1.0, 0.0)
        out_ref[:, c, :] = jnp.where(lane == ROWS + 4, live, turned[c * grid : (c + 1) * grid, :])


def gather_rows(table_ref, cell, buf, at, base, count):
    for j in range(count):
        buf[pl.ds(at + j, 1), :] = table_ref[pl.ds(cell(base + j), 1), :]


def local_groups(first, last, help_count, table_ref, cell_ref, live_ref, xyz_ref, out_ref, buf, turned, points, outs):
    slots = cell_ref.shape[0]
    slab = slots // help_count
    live = live_ref[0, 0]

    def group(g, _):
        start = pl.multiple_of(g * GROUP, GROUP)

        def block(b, _):
            off = pl.multiple_of(start + b * LANES, LANES)
            gather_rows(table_ref, lambda i: cell_ref[i], buf, 0, off, LANES)
            turned[pl.ds(pl.multiple_of(b * ROWS, ROWS), ROWS), :] = buf[...].T[0:ROWS, :]
            points[pl.ds(pl.multiple_of(b * 8, 8), 3), :] = xyz_ref[:, pl.ds(off, LANES)]
            return 0

        lax.fori_loop(0, 8, block, 0)
        values = interpolate(
            [points[pl.ds(d, 8, stride=8), :] for d in range(3)],
            lambda v: turned[pl.ds(v, 8, stride=ROWS), :],
        )
        slot = (
            start
            + lax.broadcasted_iota(jnp.int32, (8, LANES), 0) * LANES
            + lax.broadcasted_iota(jnp.int32, (8, LANES), 1)
        )
        keep = lax.rem(slot, slab) * help_count + lax.div(slot, slab) < live
        for f in range(5):
            outs[pl.ds(f, 8, stride=8), :] = jnp.where(keep, values[f], 0.0)
        for b in range(8):
            out_ref[:, pl.ds(pl.multiple_of(start + b * LANES, LANES), LANES)] = outs[pl.ds(b * 8, 5), :]
        return 0

    lax.fori_loop(first, last, group, 0)


def first_kernel(last, help_count, _, corners_ref, solution_ref, cell_ref, live_ref, xyz_ref, table_ref, out_ref, buf, turned, points, outs):
    cells = corners_ref.shape[1]

    def chunk(t, _):
        off = pl.multiple_of(t * LANES, LANES)
        both = jnp.concatenate(
            [corners_ref[:, pl.ds(off, LANES)] * 0.125, solution_ref[:, pl.ds(off, LANES)]], 0
        )
        table_ref[pl.ds(off, LANES), 0:ROWS] = both.T
        return 0

    lax.fori_loop(0, cells // LANES, chunk, 0, unroll=4)
    local_groups(0, last, help_count, table_ref, cell_ref, live_ref, xyz_ref, out_ref, buf, turned, points, outs)


def second_kernel(first, help_count, _, table_ref, cell_ref, live_ref, xyz_ref, early_ref, out_ref, buf, turned, points, outs):
    if first:
        out_ref[:, 0 : first * GROUP] = early_ref[...]
    local_groups(first, cell_ref.shape[0] // GROUP, help_count, table_ref, cell_ref, live_ref, xyz_ref, out_ref, buf, turned, points, outs)


def answer_kernel(request_ref, table_ref, out_ref, rows, cells, cell_smem, buf, sem):
    grid, depth, _ = request_ref.shape
    blocks = out_ref.shape[2] // LANES
    mine = lax.axis_index("grid")
    for c in range(depth):
        rows[pl.ds(c * grid, grid), :] = request_ref[:, c, :]
    cells[...] = rows[...].astype(jnp.int32)
    copy = pltpu.make_async_copy(cells, cell_smem, sem)
    copy.start()
    copy.wait()
    lane = lax.broadcasted_iota(jnp.int32, (LANES, LANES), 1)
    short = lane[0:8]
    for k in range(blocks):
        count = min(LANES, grid * depth - k * LANES)
        gather_rows(table_ref, lambda i: cell_smem[i, ROWS + 3], buf, 0, k * LANES, count)
        mixed = jnp.where(lane[0:count] < ROWS, buf[0:count, :], rows[k * LANES : k * LANES + count, :])
        if count < LANES:
            mixed = jnp.concatenate([mixed, jnp.zeros((LANES - count, LANES), jnp.float32)], 0)
        turned = mixed.T
        value = lambda v: turned[v : v + 1, :]
        results = interpolate([value(ROWS + d) for d in range(3)], value)
        keep = value(ROWS + 4) > 0.5
        block = jnp.concatenate(
            [jnp.where(keep, r, 0.0) for r in results] + [jnp.zeros((3, LANES), jnp.float32)], 0
        )
        here = lax.rem(short, grid) == mine

        def reply(r, _):
            moved = pltpu.roll(block, lax.rem(mine - r + LANES, LANES), 1)
            out_ref[r, :, k * LANES : (k + 1) * LANES] = jnp.where(here, moved, 0.0)
            return 0

        lax.fori_loop(0, grid, reply, 0, unroll=min(8, grid))


def per_device(help_count, corners, solution, loc_xyz, loc_cell, loc_live, rem_xyz, rem_cell, rem_count):
    grid = rem_count.shape[1]
    slots = rem_cell.shape[0]
    depth = slots // grid
    cells = corners.shape[1]
    loc = loc_cell.shape[0]
    early = (loc // GROUP) * 3 // 8
    vmem = pl.BlockSpec(memory_space=pltpu.VMEM)
    smem = pl.BlockSpec(memory_space=pltpu.SMEM)
    anyw = pl.BlockSpec(memory_space=pl.ANY)
    params = pltpu.CompilerParams(vmem_limit_bytes=VMEM_BYTES)
    scratch = [
        pltpu.VMEM((LANES, LANES), jnp.float32),
        pltpu.VMEM((8 * ROWS, LANES), jnp.float32),
        pltpu.VMEM((8 * 8, LANES), jnp.float32),
        pltpu.VMEM((8 * 8, LANES), jnp.float32),
    ]

    request = pl.pallas_call(
        request_kernel,
        out_shape=jax.ShapeDtypeStruct((grid, depth, LANES), jnp.float32),
        in_specs=[vmem] * 3,
        out_specs=vmem,
        compiler_params=params,
        name="request",
    )(rem_xyz, rem_cell.reshape(1, slots), rem_count)
    asked = lax.all_to_all(request, "grid", split_axis=0, concat_axis=0, tiled=True)
    table, early_values = pl.pallas_call(
        functools.partial(first_kernel, early, help_count),
        out_shape=(
            pltpu.VMEM((cells, LANES), jnp.float32),
            jax.ShapeDtypeStruct((5, early * GROUP), jnp.float32),
        ),
        in_specs=[anyw, vmem, vmem, smem, smem, vmem],
        out_specs=(vmem, vmem),
        scratch_shapes=scratch,
        compiler_params=params,
        cost_estimate=pl.CostEstimate(flops=1 << 24, bytes_accessed=1 << 24, transcendentals=0),
        name="local_early",
    )(request, corners, solution, loc_cell, loc_live, loc_xyz)
    width = -(-slots // LANES) * LANES
    answers = pl.pallas_call(
        answer_kernel,
        out_shape=jax.ShapeDtypeStruct((grid, 8, width), jnp.float32),
        in_specs=[vmem, vmem],
        out_specs=vmem,
        scratch_shapes=[
            pltpu.VMEM((slots, LANES), jnp.float32),
            pltpu.VMEM((slots, LANES), jnp.int32),
            pltpu.SMEM((slots, LANES), jnp.int32),
            pltpu.VMEM((LANES, LANES), jnp.float32),
            pltpu.SemaphoreType.DMA,
        ],
        compiler_params=params,
        name="answer",
    )(asked, table)
    returned = lax.all_to_all(answers, "grid", split_axis=0, concat_axis=0, tiled=True)
    loc_values = pl.pallas_call(
        functools.partial(second_kernel, early, help_count),
        out_shape=jax.ShapeDtypeStruct((5, loc), jnp.float32),
        in_specs=[anyw, vmem, smem, smem, vmem, vmem],
        out_specs=vmem,
        scratch_shapes=scratch,
        compiler_params=params,
        cost_estimate=pl.CostEstimate(flops=1 << 24, bytes_accessed=1 << 24, transcendentals=0),
        name="local_late",
    )(answers, table, loc_cell, loc_live, loc_xyz, early_values)
    rem_values = jnp.sum(returned, axis=0)[0:5, 0:slots]
    return (loc_values, rem_values)


def solution(mesh):
    placed = (
        P(None, "grid"),
        P(None, "grid"),
        P(None, ("grid", "help")),
        P(("grid", "help")),
        P("grid", "help"),
        P(None, ("grid", "help")),
        P(("grid", "help")),
        P(("grid", "help"), None),
    )
    return jax.shard_map(
        functools.partial(per_device, mesh.shape["help"]),
        mesh=mesh,
        in_specs=placed,
        out_specs=(P(None, ("grid", "help")), P(None, ("grid", "help"))),
        check_vma=False,
    )
```

time: 155 us -> 47.8 us (0.31)
  local copies, waits for them, and re-layouts: 99.6 us -> 11.1 us
  Pallas kernels: 0 us -> 20.9 us
  other arithmetic: 15.9 us -> 0.6 us
  waiting for transfers between devices: 12 us -> 0.01 us
  starting transfers between devices: 24.4 us -> 13.3 us
    gather x10 -> x0, local copies, waits for them, and re-layouts: 69.3 us -> none  [the longest x2 30.7 us: per_device(): jnp.take(results, back_index.reshape(-1), axis=1)]
    pallas_call x0 -> x4, Pallas kernels: none -> 20.9 us  [the longest x1 9.99 us: per_device(): pl.pallas_call(functools.partial(second_kernel, early, help_count), out_s...]
    all_to_all x6 -> x2, waiting for transfers between devices: 12 us -> 0.01 us  [the longest x1 0.01 us: per_device(): lax.all_to_all(request, 'grid', split_axis=0, concat_axis=0, tiled=True)]
    all_to_all x6 -> x2, starting transfers between devices: 24.4 us -> 13.3 us  [the longest x1 7.25 us: per_device(): lax.all_to_all(request, 'grid', split_axis=0, concat_axis=0, tiled=True)]
    slice x70 -> x0, local copies, waits for them, and re-layouts: 8.03 us -> none  [the longest x43 4.64 us: interpolate(): total_value = total_value + weight * fields[8 * field_idx + corner]]
    mul x10 -> x0, other arithmetic: 6.09 us -> none  [the longest x7 4.43 us: interpolate(): factors[0] * factors[1] * slopes[2]]
    squeeze x64 -> x0, local copies, waits for them, and re-layouts: 5.58 us -> none  [the longest x40 3.5 us: interpolate(): total_value = total_value + weight * fields[8 * field_idx + corner]]
    all_to_all x4 -> x0, local copies, waits for them, and re-layouts: 4.59 us -> none  [the longest x1 2.66 us: per_device(): lax.all_to_all(dealt, 'help', split_axis=1, concat_axis=1, tiled=True)]
  transfers between devices with their start and end apart: 6 -> 2, of which waited for: 4 -> 0; matrix products, arithmetic and copies ran while one was open for 22% -> 0% of each run, Pallas kernels for 0% -> 39%
where the time goes in v1:
time: 47.8 us; the launch traced here: 47.2 us
  Pallas kernels  20.9 us (44%)
  starting transfers between devices  13.3 us (28%)
  local copies, waits for them, and re-layouts  11.1 us (23%)
  between operations  1.35 us (3%)
  other arithmetic  0.6 us (1%)
    unnamed x22, local copies, waits for them, and re-layouts  11.1 us
    pallas_call x1, Pallas kernels, per_device(): pl.pallas_call(functools.partial(second_kernel, early, help_count), out_s...  9.99 us
    pallas_call x1, Pallas kernels, per_device(): pl.pallas_call(functools.partial(first_kernel, early, help_count), out_sh...  8.46 us
    all_to_all x1, starting transfers between devices, per_device(): lax.all_to_all(request, 'grid', split_axis=0, concat_axis=0, tiled=True)  7.25 us
    all_to_all x1, starting transfers between devices, per_device(): lax.all_to_all(answers, 'grid', split_axis=0, concat_axis=0, tiled=True)  6.01 us
    pallas_call x1, Pallas kernels, per_device(): pl.pallas_call(answer_kernel, out_shape=jax.ShapeDtypeStruct((grid, 8, wi...  1.71 us
  transfers between devices with their start and end apart: 2, of which 0 were waited for; matrix products, arithmetic and copies ran while one was open for 0% of the time, Pallas kernels for 39%

profile of v1, /device:TPU:0, one launch (start us, length us, event | category | flops | bytes accessed | tf_op | source)
XLA Modules:
  0.0 47.2 jit_solution(15824360713321620253)
XLA Ops:
  0.6 0.0 copy-start.7
  0.6 0.0 copy-start.8
  0.7 0.7 %copy-done.8 = f32[3,32]{1,0:T(4,128)S(1)} copy-done((f32[3,32]{1,0:T(4,128)S(1)}, f32[3,32]{1,0:T(4,128)}, u32[]{:S(2)}) %copy-start.8) | copy-done | bytes 408
  1.3 0.0 copy-start.9
  1.3 0.7 %copy-done.9 = s32[32]{0:T(128)S(1)} copy-done((s32[32]{0:T(128)S(1)}, s32[32]{0:T(128)}, u32[]{:S(2)}) %copy-start.9) | copy-done | bytes 152
  2.0 0.0 copy-start.10
  2.0 0.7 %copy-done.10 = s32[1,8]{1,0:T(1,128)S(1)} copy-done((s32[1,8]{1,0:T(1,128)S(1)}, s32[1,8]{1,0:T(1,128)}, u32[]{:S(2)}) %copy-start.10) | copy-done | bytes 56
  2.6 0.8 %request.1._ = f32[8,4,128]{2,1,0:T(4,128)} custom-call(f32[3,32]{1,0:T(4,128)S(1)} %copy-done.8, s32[1,32]{1,0:T(1,128)S(1)} %bitcast.2, s32[1,8]{1,0:T(1,128)S(1)} %copy-done.10), custom_call_target="tpu_custom_call" | custom-call | tf_op jit(solution)/shard_map/request/pallas_call | solution.py:221
  3.4 7.3 %all-to-all-start = ((f32[8,4,128]{2,1,0:T(4,128)}), f32[8,4,128]{2,1,0:T(4,128)S(1)}, u32[]{:S(2)}, u32[]{:S(2)}) async-start(f32[8,4,128]{2,1,0:T(4,128)} %request.1._), calls=%async_computation | async-start | bytes 32768 | tf_op jit(solution)/shard_map/all_to_all | solution.py:229
  11.3 0.0 copy-start.3
  11.3 1.1 %copy-done.3 = f32[24,8192]{1,0:T(8,128)S(1)} copy-done((f32[24,8192]{1,0:T(8,128)S(1)}, f32[24,8192]{1,0:T(8,128)}, u32[]{:S(2)}) %copy-start.3) | copy-done | bytes 786456
  12.4 0.0 copy-start.4
  12.4 0.9 %copy-done.4 = f32[3,8192]{1,0:T(4,128)S(1)} copy-done((f32[3,8192]{1,0:T(4,128)S(1)}, f32[3,8192]{1,0:T(4,128)}, u32[]{:S(2)}) %copy-start.4) | copy-done | bytes 98328
  13.3 0.0 copy-start.6
  13.3 0.8 %copy-done.6 = s32[8192]{0:T(1024)S(1)} copy-done((s32[8192]{0:T(1024)S(1)}, s32[8192]{0:T(1024)}, u32[]{:S(2)}) %copy-start.6) | copy-done | bytes 32792
  14.1 0.0 copy-start.5
  14.1 8.5 %local_early.1 = (f32[8192,128]{1,0:T(8,128)S(1)}, f32[5,3072]{1,0:T(8,128)S(1)}) custom-call(f32[8,4,128]{2,1,0:T(4,128)} %request.1._, f32[24,8192]{1,0:T(8,128)S(1)} %copy-done.3, f32[40,8192]{1,0:T(8,128)} %solution_ref.1, s32[8192]{0:T(1024)S(1)} %copy-done.6, s32[1,1]{1,0:T(1,128)S(6)} %copy.10.live_ref, f32[3,8192]{1,0:T(4,128)S(1)} %copy-done.4), custom_call_target="tpu_custom_call" | custom-call | flops 16777216 | bytes 16777216 | tf_op jit(solution)/shard_map/local_early/pallas_call | solution.py:230
  22.6 0.0 copy-start
  22.6 1.9 %copy-done = f32[8192,128]{1,0:T(8,128)} copy-done((f32[8192,128]{1,0:T(8,128)}, f32[8192,128]{1,0:T(8,128)S(1)}, u32[]{:S(2)}) %copy-start) | copy-done | bytes 4194328
  24.5 0.0 all-to-all-done.request_ref
  24.5 0.0 copy-start.1
  24.5 2.2 %copy-done.1 = f32[8192,128]{1,0:T(8,128)S(1)} copy-done((f32[8192,128]{1,0:T(8,128)S(1)}, f32[8192,128]{1,0:T(8,128)}, u32[]{:S(2)}) %copy-start.1) | copy-done | bytes 4194328
  26.7 1.7 %answer.1._ = f32[8,8,128]{2,1,0:T(8,128)} custom-call(f32[8,4,128]{2,1,0:T(4,128)S(1)} %all-to-all-done.request_ref, f32[8192,128]{1,0:T(8,128)S(1)} %copy-done.1), custom_call_target="tpu_custom_call" | custom-call | tf_op jit(solution)/shard_map/answer/pallas_call | solution.py:244
  28.4 6.0 %all-to-all-start.1 = ((f32[8,8,128]{2,1,0:T(8,128)}), f32[8,8,128]{2,1,0:T(8,128)S(1)}, u32[]{:S(2)}, u32[]{:S(2)}) async-start(f32[8,8,128]{2,1,0:T(8,128)} %answer.1._), calls=%async_computation.1 | async-start | bytes 65536 | tf_op jit(solution)/shard_map/all_to_all | solution.py:259
  34.4 0.0 copy-done.7
  34.4 0.0 copy-done.5
  34.5 0.0 copy-start.2
  34.5 2.2 %copy-done.2 = f32[8192,128]{1,0:T(8,128)S(1)} copy-done((f32[8192,128]{1,0:T(8,128)S(1)}, f32[8192,128]{1,0:T(8,128)}, u32[]{:S(2)}) %copy-start.2) | copy-done | bytes 4194328
  36.6 10.0 %local_late.1 = f32[5,8192]{1,0:T(8,128)} custom-call(f32[8,8,128]{2,1,0:T(8,128)} %answer.1._, f32[8192,128]{1,0:T(8,128)S(1)} %copy-done.2, s32[8192]{0:T(1024)S(1)} %copy-done.7, s32[1,1]{1,0:T(1,128)S(6)} %copy.10.live_ref, f32[3,8192]{1,0:T(4,128)S(1)} %copy-done.5, f32[5,3072]{1,0:T(8,128)S(1)} %get-tuple-element.5.early_ref), custom_call_target="tpu_custom_call" | custom-call | flops 16777216 | bytes 16777216 | tf_op jit(solution)/shard_map/local_late/pallas_call | solution.py:260
  46.6 0.0 all-to-all-done.1
  46.6 0.6 %reduce_sum.9 = f32[8,128]{1,0:T(8,128)} reduce(f32[8,8,128]{2,1,0:T(8,128)S(1)} %all-to-all-done.1, f32[]{:T(128)} %constant.0.clone.1), dimensions={0}, to_apply=%region_0.0 | reduce | flops 7168 | bytes 36868 | tf_op jit(solution)/shard_map/reduce_sum | solution.py:270
Async XLA Ops:
  0.6 33.8 %copy-start.7 = (s32[8192]{0:T(1024)S(1)}, s32[8192]{0:T(1024)}, u32[]{:S(2)}) copy-start(s32[8192]{0:T(1024)} %cell_ref.3) | copy-start | bytes 98308
  0.6 0.7 %copy-start.8 = (f32[3,32]{1,0:T(4,128)S(1)}, f32[3,32]{1,0:T(4,128)}, u32[]{:S(2)}) copy-start(f32[3,32]{1,0:T(4,128)} %xyz_ref.3) | copy-start | bytes 1156
  1.3 0.7 %copy-start.9 = (s32[32]{0:T(128)S(1)}, s32[32]{0:T(128)}, u32[]{:S(2)}) copy-start(s32[32]{0:T(128)} %param.14) | copy-start | bytes 388
  2.0 0.7 %copy-start.10 = (s32[1,8]{1,0:T(1,128)S(1)}, s32[1,8]{1,0:T(1,128)}, u32[]{:S(2)}) copy-start(s32[1,8]{1,0:T(1,128)} %count_ref.1) | copy-start | bytes 100
  3.4 21.1 %all-to-all-start = ((f32[8,4,128]{2,1,0:T(4,128)}), f32[8,4,128]{2,1,0:T(4,128)S(1)}, u32[]{:S(2)}, u32[]{:S(2)}) async-start(f32[8,4,128]{2,1,0:T(4,128)} %request.1._), calls=%async_computation | async-start | bytes 32768 | tf_op jit(solution)/shard_map/all_to_all | solution.py:229
  11.3 1.1 %copy-start.3 = (f32[24,8192]{1,0:T(8,128)S(1)}, f32[24,8192]{1,0:T(8,128)}, u32[]{:S(2)}) copy-start(f32[24,8192]{1,0:T(8,128)} %corners_ref.1) | copy-start | bytes 2359300
  12.4 0.9 %copy-start.4 = (f32[3,8192]{1,0:T(4,128)S(1)}, f32[3,8192]{1,0:T(4,128)}, u32[]{:S(2)}) copy-start(f32[3,8192]{1,0:T(4,128)} %xyz_ref.5) | copy-start | bytes 294916
  13.3 0.8 %copy-start.6 = (s32[8192]{0:T(1024)S(1)}, s32[8192]{0:T(1024)}, u32[]{:S(2)}) copy-start(s32[8192]{0:T(1024)} %cell_ref.3) | copy-start | bytes 98308
  14.1 20.3 %copy-start.5 = (f32[3,8192]{1,0:T(4,128)S(1)}, f32[3,8192]{1,0:T(4,128)}, u32[]{:S(2)}) copy-start(f32[3,8192]{1,0:T(4,128)} %xyz_ref.5) | copy-start | bytes 294916
  22.6 1.9 %copy-start = (f32[8192,128]{1,0:T(8,128)}, f32[8192,128]{1,0:T(8,128)S(1)}, u32[]{:S(2)}) copy-start(f32[8192,128]{1,0:T(8,128)S(1)} %get-tuple-element.4.table_ref) | copy-start | bytes 12582916
  24.5 2.2 %copy-start.1 = (f32[8192,128]{1,0:T(8,128)S(1)}, f32[8192,128]{1,0:T(8,128)}, u32[]{:S(2)}) copy-start(f32[8192,128]{1,0:T(8,128)} %copy-done) | copy-start | bytes 12582916
  28.4 18.2 %all-to-all-start.1 = ((f32[8,8,128]{2,1,0:T(8,128)}), f32[8,8,128]{2,1,0:T(8,128)S(1)}, u32[]{:S(2)}, u32[]{:S(2)}) async-start(f32[8,8,128]{2,1,0:T(8,128)} %answer.1._), calls=%async_computation.1 | async-start | bytes 65536 | tf_op jit(solution)/shard_map/all_to_all | solution.py:259
  34.5 2.2 %copy-start.2 = (f32[8192,128]{1,0:T(8,128)S(1)}, f32[8192,128]{1,0:T(8,128)}, u32[]{:S(2)}) copy-start(f32[8192,128]{1,0:T(8,128)} %copy-done) | copy-start | bytes 12582916

commit v2 on v1

v2 whole, which is shorter than its diff:
```python
import functools
import jax
import jax.numpy as jnp
from jax import lax
from jax.experimental import pallas as pl
from jax.experimental.pallas import tpu as pltpu
from jax.sharding import PartitionSpec as P

PASSES = 3
LANES = 128
GROUP = 8 * LANES
ROWS = 64
VMEM_BYTES = 32 << 20
EARLY = 3
LEAD = 3
QUARTERS = 4
STRIDE = 72


def monomials(corner):
    values = list(corner)
    for bit in (1, 2, 4):
        fresh = list(values)
        for k in range(8):
            if not k & bit:
                fresh[k] = values[k] + values[k | bit]
                fresh[k | bit] = values[k | bit] - values[k]
        values = fresh
    return values


def newton_step(jac, res):
    (a0, a1, a2), (b0, b1, b2), (c0, c1, c2) = jac
    k00 = b1 * c2 - b2 * c1
    k01 = b2 * c0 - b0 * c2
    k02 = b0 * c1 - b1 * c0
    k10 = a2 * c1 - a1 * c2
    k11 = a0 * c2 - a2 * c0
    k12 = a1 * c0 - a0 * c1
    k20 = a1 * b2 - a2 * b1
    k21 = a2 * b0 - a0 * b2
    k22 = a0 * b1 - a1 * b0
    inverse = 1.0 / (a0 * k00 + a1 * k01 + a2 * k02)
    return (
        (k00 * res[0] + k10 * res[1] + k20 * res[2]) * inverse,
        (k01 * res[0] + k11 * res[1] + k21 * res[2]) * inverse,
        (k02 * res[0] + k12 * res[1] + k22 * res[2]) * inverse,
    )


def newton(points, coef):
    step = newton_step(
        [[coef(i, 1), coef(i, 2), coef(i, 4)] for i in range(3)],
        [coef(i, 0) - points[i] for i in range(3)],
    )
    xi = [-s for s in step]
    for _ in range(PASSES - 1):
        x, y, z = xi
        jac, res = [], []
        for i in range(3):
            a0 = coef(i, 0) + coef(i, 4) * z
            a1 = coef(i, 1) + coef(i, 5) * z
            a2 = coef(i, 2) + coef(i, 6) * z
            a3 = coef(i, 3) + coef(i, 7) * z
            dx = a1 + a3 * y
            dy = a2 + a3 * x
            dz = (coef(i, 4) + coef(i, 6) * y) + (coef(i, 5) + coef(i, 7) * y) * x
            jac.append([dx, dy, dz])
            res.append((a0 + a2 * y) + dx * x - points[i])
        step = newton_step(jac, res)
        xi = [xi[d] - step[d] for d in range(3)]
    return xi


def blend(xi, value):
    low = [0.5 - 0.5 * v for v in xi]
    high = [0.5 + 0.5 * v for v in xi]
    plane = [p * q for q in (low[1], high[1]) for p in (low[0], high[0])]
    weights = [w * q for q in (low[2], high[2]) for w in plane]
    outs = []
    for f in range(5):
        total = weights[0] * value(24 + 8 * f)
        for k in range(1, 8):
            total = total + weights[k] * value(24 + 8 * f + k)
        outs.append(total)
    return outs


def wait_all(copies):
    for c in copies:
        c.start()
    for c in copies:
        c.wait()


def request_kernel(lead, xyz_hbm, cell_hbm, count_hbm, out_ref, xyz_ref, cell_ref, count_ref, sems):
    wait_all(
        [
            pltpu.make_async_copy(xyz_hbm, xyz_ref, sems.at[0]),
            pltpu.make_async_copy(cell_hbm, cell_ref, sems.at[1]),
            pltpu.make_async_copy(count_hbm, count_ref, sems.at[2]),
        ]
    )
    grid, depth, _ = out_ref.shape
    slots = xyz_ref.shape[1]
    width = -(-slots // LANES) * LANES
    wide = lambda a: a if a.shape[1] == width else jnp.pad(a, ((0, 0), (0, width - a.shape[1])))
    stack = jnp.concatenate(
        [
            jnp.zeros((ROWS, width), jnp.float32),
            wide(xyz_ref[...]),
            wide(cell_ref[...].astype(jnp.float32)),
            wide(count_ref[...].astype(jnp.float32)),
            jnp.zeros((LANES - ROWS - 5, width), jnp.float32),
        ],
        0,
    )
    turned = jnp.concatenate(
        [stack[:, k : k + LANES].T for k in range(0, width, LANES)], 0
    )
    counts = turned[0:grid, ROWS + 4 : ROWS + 5]
    lane = lax.broadcasted_iota(jnp.int32, (grid, LANES), 1)
    for c in range(depth):
        live = jnp.where(counts > float(c), 1.0, 0.0)
        whole = jnp.where(lane == ROWS + 4, live, turned[c * grid : (c + 1) * grid, :])
        out_ref[:, c, :] = jnp.concatenate([whole[lead:], whole[:lead]], 0) if lead else whole


class Local:
    @staticmethod
    def scratch(cells, groups):
        return [
            pltpu.VMEM((cells, LANES), jnp.float32),
            *[pltpu.SMEM((2, LANES), jnp.int32)] * QUARTERS,
            *[pltpu.VMEM((LANES, LANES), jnp.float32)] * QUARTERS,
            pltpu.VMEM(((groups + 1) * 8 * STRIDE, LANES), jnp.float32),
            pltpu.VMEM((24, 8, LANES), jnp.float32),
            pltpu.VMEM((3, 8, LANES), jnp.float32),
            pltpu.VMEM((64, LANES), jnp.float32),
            pltpu.VMEM((64, LANES), jnp.float32),
            pltpu.SemaphoreType.DMA((QUARTERS,)),
        ]

    def __init__(self, first, last, help_count, rows, live, xyz, stage, finished, *scratch):
        self.first, self.last, self.help_count = first, last, help_count
        self.rows, self.live, self.xyz, self.stage, self.finished = rows, live, xyz, stage, finished
        self.wide = scratch[0]
        self.smem, self.buf = scratch[1 : 1 + QUARTERS], scratch[1 + QUARTERS : 1 + 2 * QUARTERS]
        (self.turned, self.coefs, self.xi, self.points, self.outs, self.row_sems) = scratch[1 + 2 * QUARTERS :]

    def fetch(self, q, k):
        return pltpu.make_async_copy(self.rows.at[pl.ds(2 * (QUARTERS * self.first + q), 2), :], self.smem[k], self.row_sems.at[k])

    def turn(self, q, k):
        block = self.buf[k][...].T
        for h in range(2):
            at = pl.multiple_of((2 * q + 8 + h) * STRIDE, 8)
            self.turned[pl.ds(at, ROWS), :] = block[h * ROWS : (h + 1) * ROWS, :]

    def gather(self, k):
        for h in range(2):
            lanes = slice(h * ROWS, (h + 1) * ROWS)
            for j in range(LANES):
                self.buf[k][j : j + 1, lanes] = self.wide[pl.ds(self.smem[k][h, j], 1), lanes]

    def begin(self):
        for k in range(QUARTERS):
            self.fetch(k, k).start()

    def run(self):
        groups = self.last - self.first
        stages = (lambda g: None, self.expand, self.solve, self.fields)

        def group(g, _):
            for k in range(QUARTERS):
                q = QUARTERS * g + k
                self.fetch(q, k).wait()
                self.gather(k)
                stages[k](g - 1)
                self.turn(q - 1, (k - 1) % QUARTERS)

                @pl.when(g + 1 < groups)
                def _():
                    self.fetch(q + QUARTERS, k).start()

            @pl.when(g > 0)
            def _():
                self.finished(g - 1)

            return 0

        lax.fori_loop(0, groups, group, 0)
        self.turn(QUARTERS * groups - 1, QUARTERS - 1)
        for stage in stages:
            stage(groups - 1)
        self.finished(groups - 1)

    def value(self, g, v):
        return self.turned[pl.ds((g + 1) * 8 * STRIDE + v, 8, stride=STRIDE), :]

    def expand(self, g):
        for i in range(3):
            for k, c in enumerate(monomials([self.value(g, 8 * i + k) for k in range(8)])):
                self.coefs[8 * i + k] = c
        for b in range(8):
            at = pl.multiple_of(jnp.maximum(self.first + g, 0) * GROUP + b * LANES, LANES)
            self.points[b * 8 : b * 8 + 3, :] = self.xyz[:, pl.ds(at, LANES)]

    def solve(self, g):
        xi = newton(
            [self.points[pl.ds(d, 8, stride=8), :] for d in range(3)],
            lambda i, k: self.coefs[8 * i + k],
        )
        for d in range(3):
            self.xi[d] = xi[d]

    def fields(self, g):
        values = blend([self.xi[d] for d in range(3)], lambda v: self.value(g, v))
        slab = self.xyz.shape[1] // self.help_count
        slot = (
            (self.first + g) * GROUP
            + lax.broadcasted_iota(jnp.int32, (8, LANES), 0) * LANES
            + lax.broadcasted_iota(jnp.int32, (8, LANES), 1)
        )
        keep = lax.rem(slot, slab) * self.help_count + lax.div(slot, slab) < self.live[...]
        for f in range(5):
            self.outs[pl.ds(f, 8, stride=8), :] = jnp.where(keep, values[f], 0.0)
        for b in range(8):
            at = pl.multiple_of((g + 1) * GROUP + b * LANES, LANES)
            self.stage[:, pl.ds(at, LANES)] = self.outs[b * 8 : b * 8 + 5, :]


PIECES = 4


def first_kernel(last, help_count, _, corners_hbm, solution_hbm, cells_hbm, live_hbm, xyz_hbm, table, rows, live, xyz, stage, corners, solution, cells, live_one, sems, *scratch):
    local = Local(0, last, help_count, rows, live, xyz, stage, lambda g: None, *scratch)
    half = table.shape[0]
    piece = half // PIECES
    pieces = []
    for k in range(PIECES):
        for h in range(2):
            at = pl.ds(h * half + k * piece, piece)
            pieces.append(
                (
                    pltpu.make_async_copy(corners_hbm.at[:, at], corners.at[:, at], sems.at[4 * k + 2 * h]),
                    pltpu.make_async_copy(solution_hbm.at[:, at], solution.at[:, at], sems.at[4 * k + 2 * h + 1]),
                )
            )
    small = [
        pltpu.make_async_copy(cells_hbm, cells, sems.at[4 * PIECES]),
        pltpu.make_async_copy(xyz_hbm, xyz, sems.at[4 * PIECES + 1]),
        pltpu.make_async_copy(live_hbm, live_one, sems.at[4 * PIECES + 2]),
    ]
    for c in [c for pair in pieces for c in pair] + small:
        c.start()
    for k in range(PIECES):
        for c in pieces[2 * k] + pieces[2 * k + 1]:
            c.wait()

        def chunk(t, _):
            low = pl.multiple_of(k * piece + t * LANES, LANES)
            high = pl.multiple_of(half + low, LANES)
            both = jnp.concatenate(
                [
                    corners[:, pl.ds(low, LANES)] * 0.125,
                    solution[:, pl.ds(low, LANES)],
                    corners[:, pl.ds(high, LANES)] * 0.125,
                    solution[:, pl.ds(high, LANES)],
                ],
                0,
            ).T
            table[pl.ds(low, LANES), :] = both
            local.wide[pl.ds(low, LANES), :] = both
            local.wide[pl.ds(high, LANES), :] = pltpu.roll(both, ROWS, 1)
            return 0

        lax.fori_loop(0, piece // LANES, chunk, 0, unroll=min(8, piece // LANES))
    for c in small:
        c.wait()
    whole = cells[...]
    other = jnp.where(whole >= half, whole - half, whole + half)
    odd = lax.rem(lax.broadcasted_iota(jnp.int32, whole.shape, 0), 2) == 1
    rows[...] = jnp.where(odd, other, whole)
    live[...] = jnp.broadcast_to(live_one[...], live.shape)
    local.begin()
    local.run()


def second_kernel(first, last, help_count, _, table, rows, live, xyz, early, loc_hbm, stage, out_sems, *scratch):
    def result(g):
        return pltpu.make_async_copy(
            stage.at[:, pl.ds(pl.multiple_of((g + 1) * GROUP, GROUP), GROUP)],
            loc_hbm.at[:, pl.ds(pl.multiple_of((first + g) * GROUP, GROUP), GROUP)],
            out_sems.at[g],
        )

    part = pl.ds(GROUP, first * GROUP)
    before = pltpu.make_async_copy(early.at[:, part], loc_hbm.at[:, pl.ds(0, first * GROUP)], out_sems.at[last - first])
    before.start()
    local = Local(first, last, help_count, rows, live, xyz, stage, lambda g: result(g).start(), *scratch)
    local.begin()
    half = table.shape[0]

    def chunk(t, _):
        at = pl.multiple_of(t * LANES, LANES)
        both = table[pl.ds(at, LANES), :]
        local.wide[pl.ds(at, LANES), :] = both
        local.wide[pl.ds(pl.multiple_of(half + at, LANES), LANES), :] = pltpu.roll(both, ROWS, 1)
        return 0

    lax.fori_loop(0, half // LANES, chunk, 0, unroll=2)
    local.run()
    before.wait()
    for g in range(last - first):
        result(g).wait()


def answer_kernel(request_ref, table_ref, out_ref, rows, cells, cell_smem, buf, sem):
    grid, depth, _ = request_ref.shape
    half = table_ref.shape[0]
    blocks = out_ref.shape[2] // LANES
    mine = lax.axis_index("grid")
    for c in range(depth):
        rows[pl.ds(c * grid, grid), :] = request_ref[:, c, :]
    number = rows[...].astype(jnp.int32)
    cells[...] = jnp.where(number >= half, number - half, number)
    copy = pltpu.make_async_copy(cells, cell_smem, sem)
    copy.start()
    copy.wait()
    lane = lax.broadcasted_iota(jnp.int32, (LANES, LANES), 1)
    short = lane[0:8]
    for k in range(blocks):
        count = min(LANES, grid * depth - k * LANES)
        for j in range(count):
            buf[j : j + 1, :] = table_ref[pl.ds(cell_smem[k * LANES + j, ROWS + 3], 1), :]
        turned = buf[...].T
        asked = rows[k * LANES : k * LANES + count, :]
        if count < LANES:
            asked = jnp.concatenate([asked, jnp.zeros((LANES - count, LANES), jnp.float32)], 0)
        asked = asked.T[ROWS : ROWS + 8, :]
        upper = asked[3:4, :] >= float(half)
        value = lambda v: jnp.where(upper, turned[ROWS + v : ROWS + v + 1, :], turned[v : v + 1, :])
        coefs = [monomials([value(8 * i + k) for k in range(8)]) for i in range(3)]
        xi = newton([asked[d : d + 1, :] for d in range(3)], lambda i, k: coefs[i][k])
        results = blend(xi, value)
        keep = asked[4:5, :] > 0.5
        block = jnp.concatenate(
            [jnp.where(keep, r, 0.0) for r in results] + [jnp.zeros((3, LANES), jnp.float32)], 0
        )
        here = lax.rem(short, grid) == mine

        def reply(r, _):
            moved = pltpu.roll(block, lax.rem(mine - r + LANES, LANES), 1)
            out_ref[r, :, k * LANES : (k + 1) * LANES] = jnp.where(here, moved, 0.0)
            return 0

        lax.fori_loop(0, grid, reply, 0, unroll=min(8, grid))


def per_device(help_count, corners, solution, loc_xyz, loc_cell, loc_live, rem_xyz, rem_cell, rem_count):
    grid = rem_count.shape[1]
    slots = rem_cell.shape[0]
    depth = slots // grid
    cells = corners.shape[1]
    loc = loc_cell.shape[0]
    early = EARLY
    lead = grid * LEAD // 8
    exchange = functools.partial(
        lax.all_to_all,
        axis_name="grid",
        split_axis=0,
        concat_axis=0,
        axis_index_groups=[[(j + lead) % grid for j in range(grid)]],
        tiled=True,
    )
    vmem = pl.BlockSpec(memory_space=pltpu.VMEM)
    hbm = pl.BlockSpec(memory_space=pltpu.HBM)
    anyw = pl.BlockSpec(memory_space=pl.ANY)
    params = pltpu.CompilerParams(vmem_limit_bytes=VMEM_BYTES)
    far = lambda a: pltpu.with_memory_space_constraint(a, pltpu.HBM)
    corners, solution, loc_xyz, rem_xyz, rem_count = map(far, (corners, solution, loc_xyz, rem_xyz, rem_count))
    cells2d = far(loc_cell.reshape(loc // LANES, LANES))
    rem_cell = far(rem_cell.reshape(1, slots))

    request = pl.pallas_call(
        functools.partial(request_kernel, lead),
        out_shape=jax.ShapeDtypeStruct((grid, depth, LANES), jnp.float32),
        in_specs=[hbm] * 3,
        out_specs=vmem,
        scratch_shapes=[
            pltpu.VMEM((3, slots), jnp.float32),
            pltpu.VMEM((1, slots), jnp.int32),
            pltpu.VMEM((1, grid), jnp.int32),
            pltpu.SemaphoreType.DMA((3,)),
        ],
        compiler_params=params,
        name="request",
    )(rem_xyz, rem_cell, rem_count)
    asked = exchange(request)
    table, rows, live, xyz, loc_early = pl.pallas_call(
        functools.partial(first_kernel, early, help_count),
        out_shape=(
            pltpu.VMEM((cells // 2, LANES), jnp.float32),
            pltpu.VMEM((loc // LANES, LANES), jnp.int32),
            pltpu.VMEM((8, LANES), jnp.int32),
            pltpu.VMEM((3, loc), jnp.float32),
            pltpu.VMEM((5, (early + 1) * GROUP), jnp.float32),
        ),
        in_specs=[anyw] + [hbm] * 5,
        out_specs=(vmem,) * 5,
        scratch_shapes=[
            pltpu.VMEM((24, cells), jnp.float32),
            pltpu.VMEM((40, cells), jnp.float32),
            pltpu.VMEM((loc // LANES, LANES), jnp.int32),
            pltpu.VMEM((1, 1), jnp.int32),
            pltpu.SemaphoreType.DMA((4 * PIECES + 3,)),
            *Local.scratch(cells, early),
        ],
        compiler_params=params,
        cost_estimate=pl.CostEstimate(flops=1 << 24, bytes_accessed=1 << 24, transcendentals=0),
        name="local_early",
    )(request, corners, solution, cells2d, loc_live, loc_xyz)
    width = -(-slots // LANES) * LANES
    answers = pl.pallas_call(
        answer_kernel,
        out_shape=jax.ShapeDtypeStruct((grid, 8, width), jnp.float32),
        in_specs=[vmem, vmem],
        out_specs=vmem,
        scratch_shapes=[
            pltpu.VMEM((slots, LANES), jnp.float32),
            pltpu.VMEM((slots, LANES), jnp.int32),
            pltpu.SMEM((slots, LANES), jnp.int32),
            pltpu.VMEM((LANES, LANES), jnp.float32),
            pltpu.SemaphoreType.DMA,
        ],
        compiler_params=params,
        name="answer",
    )(asked, table)
    returned = exchange(answers)
    late = loc // GROUP - early
    loc_values = pl.pallas_call(
        functools.partial(second_kernel, early, loc // GROUP, help_count),
        out_shape=jax.ShapeDtypeStruct((5, loc), jnp.float32),
        in_specs=[anyw] + [vmem] * 5,
        out_specs=hbm,
        scratch_shapes=[
            pltpu.VMEM((5, (late + 1) * GROUP), jnp.float32),
            pltpu.SemaphoreType.DMA((late + 1,)),
            *Local.scratch(cells, late),
        ],
        compiler_params=params,
        cost_estimate=pl.CostEstimate(flops=1 << 24, bytes_accessed=1 << 24, transcendentals=0),
        name="local_late",
    )(answers, table, rows, live, xyz, loc_early)
    rem_values = jnp.sum(returned, axis=0)[0:5, 0:slots]
    return (loc_values, rem_values)


def solution(mesh):
    placed = (
        P(None, "grid"),
        P(None, "grid"),
        P(None, ("grid", "help")),
        P(("grid", "help")),
        P("grid", "help"),
        P(None, ("grid", "help")),
        P(("grid", "help")),
        P(("grid", "help"), None),
    )
    return jax.shard_map(
        functools.partial(per_device, mesh.shape["help"]),
        mesh=mesh,
        in_specs=placed,
        out_specs=(P(None, ("grid", "help")), P(None, ("grid", "help"))),
        check_vma=False,
    )
```

time: 47.8 us -> 30.2 us (0.63)
  local copies, waits for them, and re-layouts: 11.1 us -> 0 us
  Pallas kernels: 20.9 us -> 15 us
    unnamed x22 -> x0, local copies, waits for them, and re-layouts: 11.1 us -> none
    pallas_call x2, Pallas kernels: 10.7 us -> 7.51 us  [the longest x1 6.05 us: per_device(): pl.pallas_call(functools.partial(second_kernel, early, loc // GROUP, help...]
    pallas_call x1, Pallas kernels: 8.46 us -> 5.77 us  [per_device(): pl.pallas_call(functools.partial(first_kernel, early, help_count), out_sh...]
  transfers between devices with their start and end apart: 2 -> 2, of which waited for: 0 -> 0; matrix products, arithmetic and copies ran while one was open for 0% -> 0% of each run, Pallas kernels for 39% -> 40%
where the time goes in v2:
time: 30.2 us; the launch traced here: 29.9 us
  Pallas kernels  15 us (50%)
  starting transfers between devices  12.9 us (43%)
  between operations  1.33 us (4%)
  other arithmetic  0.6 us (2%)
    all_to_all x1, starting transfers between devices, per_device(): asked = exchange(request)  7.83 us
    pallas_call x1, Pallas kernels, per_device(): pl.pallas_call(functools.partial(second_kernel, early, loc // GROUP, help...  6.05 us
    pallas_call x1, Pallas kernels, per_device(): pl.pallas_call(functools.partial(first_kernel, early, help_count), out_sh...  5.77 us
    all_to_all x1, starting transfers between devices, per_device(): returned = exchange(answers)  5.11 us
    pallas_call x1, Pallas kernels, per_device(): pl.pallas_call(answer_kernel, out_shape=jax.ShapeDtypeStruct((grid, 8, wi...  1.72 us
    pallas_call x1, Pallas kernels, per_device(): pl.pallas_call(functools.partial(request_kernel, lead), out_shape=jax.Sha...  1.47 us
  transfers between devices with their start and end apart: 2, of which 0 were waited for; matrix products, arithmetic and copies ran while one was open for 0% of the time, Pallas kernels for 40%

profile of v2, /device:TPU:0, one launch (start us, length us, event | category | flops | bytes accessed | tf_op | source)
XLA Modules:
  0.0 29.9 jit_solution(17391660601993408335)
XLA Ops:
  0.6 1.5 %request.1._ = f32[8,4,128]{2,1,0:T(4,128)} custom-call(f32[3,32]{1,0:T(4,128)} %xyz_hbm.2, s32[1,32]{1,0:T(1,128)} %bitcast.5, s32[1,8]{1,0:T(1,128)} %count_hbm.1), custom_call_target="tpu_custom_call" | custom-call | tf_op jit(solution)/shard_map/request/pallas_call | solution.py:386
  2.1 7.8 %all-to-all-start = ((f32[8,4,128]{2,1,0:T(4,128)}), f32[8,4,128]{2,1,0:T(4,128)S(1)}, u32[]{:S(2)}, u32[]{:S(2)}) async-start(f32[8,4,128]{2,1,0:T(4,128)} %request.1._), calls=%async_computation | async-start | bytes 32768 | tf_op jit(solution)/shard_map/all_to_all | solution.py:400
  10.6 5.8 %local_early.1 = (f32[4096,128]{1,0:T(8,128)S(1)}, s32[64,128]{1,0:T(8,128)S(1)}, s32[8,128]{1,0:T(8,128)S(1)}, f32[3,8192]{1,0:T(4,128)S(1)}, f32[5,4096]{1,0:T(8,128)S(1)}) custom-call(f32[8,4,128]{2,1,0:T(4,128)} %request.1._, f32[24,8192]{1,0:T(8,128)} %corners_hbm.1, f32[40,8192]{1,0:T(8,128)} %solution_hbm.1, s32[64,128]{1,0:T(8,128)} %bitcast.3, ...), custom_call_target="tpu_custom_call" | custom-call | flops 16777216 | bytes 16777216 | tf_op jit(solution)/shard_map/local_early/pallas_call | solution.py:401
  16.4 0.0 all-to-all-done.request_ref
  16.4 1.7 %answer.1._ = f32[8,8,128]{2,1,0:T(8,128)} custom-call(f32[8,4,128]{2,1,0:T(4,128)S(1)} %all-to-all-done.request_ref, f32[4096,128]{1,0:T(8,128)S(1)} %get-tuple-element.7.table_ref.table), custom_call_target="tpu_custom_call" | custom-call | tf_op jit(solution)/shard_map/answer/pallas_call | solution.py:425
  18.1 5.1 %all-to-all-start.1 = ((f32[8,8,128]{2,1,0:T(8,128)}), f32[8,8,128]{2,1,0:T(8,128)S(1)}, u32[]{:S(2)}, u32[]{:S(2)}) async-start(f32[8,8,128]{2,1,0:T(8,128)} %answer.1._), calls=%async_computation.1 | async-start | bytes 65536 | tf_op jit(solution)/shard_map/all_to_all | solution.py:440
  23.2 6.0 %local_late.1 = f32[5,8192]{1,0:T(8,128)} custom-call(f32[8,8,128]{2,1,0:T(8,128)} %answer.1._, f32[4096,128]{1,0:T(8,128)S(1)} %get-tuple-element.7.table_ref.table, s32[64,128]{1,0:T(8,128)S(1)} %get-tuple-element.8.rows, s32[8,128]{1,0:T(8,128)S(1)} %get-tuple-element.9.live, f32[3,8192]{1,0:T(4,128)S(1)} %get-tuple-element.10.xyz, ...), custom_call_target="tpu_custom_call" | custom-call | flops 16777216 | bytes 16777216 | tf_op jit(solution)/shard_map/local_late/pallas_call | solution.py:442
  29.3 0.0 all-to-all-done.1
  29.3 0.6 %reduce_sum.9 = f32[8,128]{1,0:T(8,128)} reduce(f32[8,8,128]{2,1,0:T(8,128)S(1)} %all-to-all-done.1, f32[]{:T(128)} %constant.0.clone.1), dimensions={0}, to_apply=%region_0.0 | reduce | flops 7168 | bytes 36868 | tf_op jit(solution)/shard_map/reduce_sum | solution.py:456
Async XLA Ops:
  2.1 14.3 %all-to-all-start = ((f32[8,4,128]{2,1,0:T(4,128)}), f32[8,4,128]{2,1,0:T(4,128)S(1)}, u32[]{:S(2)}, u32[]{:S(2)}) async-start(f32[8,4,128]{2,1,0:T(4,128)} %request.1._), calls=%async_computation | async-start | bytes 32768 | tf_op jit(solution)/shard_map/all_to_all | solution.py:400
  18.1 11.2 %all-to-all-start.1 = ((f32[8,8,128]{2,1,0:T(8,128)}), f32[8,8,128]{2,1,0:T(8,128)S(1)}, u32[]{:S(2)}, u32[]{:S(2)}) async-start(f32[8,8,128]{2,1,0:T(8,128)} %answer.1._), calls=%async_computation.1 | async-start | bytes 65536 | tf_op jit(solution)/shard_map/all_to_all | solution.py:440

commit v3 on v2

--- a/solution.py
+++ b/solution.py
@@ -13,6 +13,7 @@
 VMEM_BYTES = 32 << 20
 EARLY = 3
 LEAD = 3
+WIDEN = 16
 QUARTERS = 4
 STRIDE = 72
 
@@ -152,10 +153,11 @@
         return pltpu.make_async_copy(self.rows.at[pl.ds(2 * (QUARTERS * self.first + q), 2), :], self.smem[k], self.row_sems.at[k])
 
     def turn(self, q, k):
-        block = self.buf[k][...].T
-        for h in range(2):
-            at = pl.multiple_of((2 * q + 8 + h) * STRIDE, 8)
-            self.turned[pl.ds(at, ROWS), :] = block[h * ROWS : (h + 1) * ROWS, :]
+        blocks = [self.buf[k + i][...].T for i in range(2)]
+        for i in range(2):
+            for h in range(2):
+                at = pl.multiple_of((2 * (q + i) + 8 + h) * STRIDE, 8)
+                self.turned[pl.ds(at, ROWS), :] = blocks[i][h * ROWS : (h + 1) * ROWS, :]
 
     def gather(self, k):
         for h in range(2):
@@ -177,7 +179,8 @@
                 self.fetch(q, k).wait()
                 self.gather(k)
                 stages[k](g - 1)
-                self.turn(q - 1, (k - 1) % QUARTERS)
+                if k % 2 == 0:
+                    self.turn(q - 2, (k - 2) % QUARTERS)
 
                 @pl.when(g + 1 < groups)
                 def _():
@@ -190,7 +193,7 @@
             return 0
 
         lax.fori_loop(0, groups, group, 0)
-        self.turn(QUARTERS * groups - 1, QUARTERS - 1)
+        self.turn(QUARTERS * groups - 2, QUARTERS - 2)
         for stage in stages:
             stage(groups - 1)
         self.finished(groups - 1)
@@ -230,7 +233,7 @@
             self.stage[:, pl.ds(at, LANES)] = self.outs[b * 8 : b * 8 + 5, :]
 
 
-PIECES = 4
+PIECES = 2
 
 
 def first_kernel(last, help_count, _, corners_hbm, solution_hbm, cells_hbm, live_hbm, xyz_hbm, table, rows, live, xyz, stage, corners, solution, cells, live_one, sems, *scratch):
@@ -252,8 +255,14 @@
         pltpu.make_async_copy(xyz_hbm, xyz, sems.at[4 * PIECES + 1]),
         pltpu.make_async_copy(live_hbm, live_one, sems.at[4 * PIECES + 2]),
     ]
-    for c in [c for pair in pieces for c in pair] + small:
+    for c in small[:1] + [c for pair in pieces for c in pair] + small[1:]:
         c.start()
+    small[0].wait()
+    whole = cells[...]
+    other = jnp.where(whole >= half, whole - half, whole + half)
+    odd = lax.rem(lax.broadcasted_iota(jnp.int32, whole.shape, 0), 2) == 1
+    rows[...] = jnp.where(odd, other, whole)
+    local.begin()
     for k in range(PIECES):
         for c in pieces[2 * k] + pieces[2 * k + 1]:
             c.wait()
@@ -275,30 +284,19 @@
             local.wide[pl.ds(high, LANES), :] = pltpu.roll(both, ROWS, 1)
             return 0
 
-        lax.fori_loop(0, piece // LANES, chunk, 0, unroll=min(8, piece // LANES))
-    for c in small:
+        lax.fori_loop(0, piece // LANES, chunk, 0, unroll=min(16, piece // LANES))
+    for c in small[1:]:
         c.wait()
-    whole = cells[...]
-    other = jnp.where(whole >= half, whole - half, whole + half)
-    odd = lax.rem(lax.broadcasted_iota(jnp.int32, whole.shape, 0), 2) == 1
-    rows[...] = jnp.where(odd, other, whole)
     live[...] = jnp.broadcast_to(live_one[...], live.shape)
-    local.begin()
     local.run()
 
 
-def second_kernel(first, last, help_count, _, table, rows, live, xyz, early, loc_hbm, stage, out_sems, *scratch):
-    def result(g):
-        return pltpu.make_async_copy(
-            stage.at[:, pl.ds(pl.multiple_of((g + 1) * GROUP, GROUP), GROUP)],
-            loc_hbm.at[:, pl.ds(pl.multiple_of((first + g) * GROUP, GROUP), GROUP)],
-            out_sems.at[g],
-        )
-
-    part = pl.ds(GROUP, first * GROUP)
-    before = pltpu.make_async_copy(early.at[:, part], loc_hbm.at[:, pl.ds(0, first * GROUP)], out_sems.at[last - first])
+def second_kernel(first, last, help_count, _, table, rows, live, xyz, early, loc_hbm, stage, out_sem, *scratch):
+    before = pltpu.make_async_copy(
+        early.at[:, pl.ds(GROUP, first * GROUP)], loc_hbm.at[:, pl.ds(0, first * GROUP)], out_sem
+    )
     before.start()
-    local = Local(first, last, help_count, rows, live, xyz, stage, lambda g: result(g).start(), *scratch)
+    local = Local(first, last, help_count, rows, live, xyz, stage, lambda g: None, *scratch)
     local.begin()
     half = table.shape[0]
 
@@ -309,11 +307,23 @@
         local.wide[pl.ds(pl.multiple_of(half + at, LANES), LANES), :] = pltpu.roll(both, ROWS, 1)
         return 0
 
-    lax.fori_loop(0, half // LANES, chunk, 0, unroll=2)
+    lax.fori_loop(0, half // LANES, chunk, 0, unroll=WIDEN)
     local.run()
     before.wait()
-    for g in range(last - first):
-        result(g).wait()
+
+
+def final_kernel(first, _, stage, returned, before_hbm, loc_hbm, rem_hbm, total, sems):
+    loc = pltpu.make_async_copy(
+        stage.at[:, pl.ds(GROUP, stage.shape[1] - GROUP)],
+        loc_hbm.at[:, pl.ds(first * GROUP, stage.shape[1] - GROUP)],
+        sems.at[0],
+    )
+    loc.start()
+    total[...] = jnp.sum(returned[...], axis=0)[0:5, 0 : total.shape[1]]
+    rem = pltpu.make_async_copy(total, rem_hbm, sems.at[1])
+    rem.start()
+    loc.wait()
+    rem.wait()
 
 
 def answer_kernel(request_ref, table_ref, out_ref, rows, cells, cell_smem, buf, sem):
@@ -323,22 +333,24 @@
     mine = lax.axis_index("grid")
     for c in range(depth):
         rows[pl.ds(c * grid, grid), :] = request_ref[:, c, :]
-    number = rows[...].astype(jnp.int32)
-    cells[...] = jnp.where(number >= half, number - half, number)
+    asked_all = []
+    for k in range(blocks):
+        count = min(LANES, grid * depth - k * LANES)
+        asked = rows[k * LANES : k * LANES + count, :]
+        if count < LANES:
+            asked = jnp.concatenate([asked, jnp.zeros((LANES - count, LANES), jnp.float32)], 0)
+        asked_all.append(asked.T[ROWS : ROWS + 8, :])
+        number = asked_all[k][3:4, :].astype(jnp.int32)
+        cells[k : k + 1, :] = jnp.where(number >= half, number - half, number)
     copy = pltpu.make_async_copy(cells, cell_smem, sem)
     copy.start()
     copy.wait()
-    lane = lax.broadcasted_iota(jnp.int32, (LANES, LANES), 1)
-    short = lane[0:8]
+    lane = lax.broadcasted_iota(jnp.int32, (8, LANES), 1)
     for k in range(blocks):
-        count = min(LANES, grid * depth - k * LANES)
-        for j in range(count):
-            buf[j : j + 1, :] = table_ref[pl.ds(cell_smem[k * LANES + j, ROWS + 3], 1), :]
+        for j in range(min(LANES, grid * depth - k * LANES)):
+            buf[j : j + 1, :] = table_ref[pl.ds(cell_smem[k, j], 1), :]
         turned = buf[...].T
-        asked = rows[k * LANES : k * LANES + count, :]
-        if count < LANES:
-            asked = jnp.concatenate([asked, jnp.zeros((LANES - count, LANES), jnp.float32)], 0)
-        asked = asked.T[ROWS : ROWS + 8, :]
+        asked = asked_all[k]
         upper = asked[3:4, :] >= float(half)
         value = lambda v: jnp.where(upper, turned[ROWS + v : ROWS + v + 1, :], turned[v : v + 1, :])
         coefs = [monomials([value(8 * i + k) for k in range(8)]) for i in range(3)]
@@ -348,7 +360,7 @@
         block = jnp.concatenate(
             [jnp.where(keep, r, 0.0) for r in results] + [jnp.zeros((3, LANES), jnp.float32)], 0
         )
-        here = lax.rem(short, grid) == mine
+        here = lax.rem(lane, grid) == mine
 
         def reply(r, _):
             moved = pltpu.roll(block, lax.rem(mine - r + LANES, LANES), 1)
@@ -429,8 +441,8 @@
         out_specs=vmem,
         scratch_shapes=[
             pltpu.VMEM((slots, LANES), jnp.float32),
-            pltpu.VMEM((slots, LANES), jnp.int32),
-            pltpu.SMEM((slots, LANES), jnp.int32),
+            pltpu.VMEM((width // LANES, LANES), jnp.int32),
+            pltpu.SMEM((width // LANES, LANES), jnp.int32),
             pltpu.VMEM((LANES, LANES), jnp.float32),
             pltpu.SemaphoreType.DMA,
         ],
@@ -439,21 +451,32 @@
     )(asked, table)
     returned = exchange(answers)
     late = loc // GROUP - early
-    loc_values = pl.pallas_call(
+    loc_part, stage = pl.pallas_call(
         functools.partial(second_kernel, early, loc // GROUP, help_count),
-        out_shape=jax.ShapeDtypeStruct((5, loc), jnp.float32),
+        out_shape=(
+            jax.ShapeDtypeStruct((5, loc), jnp.float32),
+            pltpu.VMEM((5, (late + 1) * GROUP), jnp.float32),
+        ),
         in_specs=[anyw] + [vmem] * 5,
-        out_specs=hbm,
-        scratch_shapes=[
-            pltpu.VMEM((5, (late + 1) * GROUP), jnp.float32),
-            pltpu.SemaphoreType.DMA((late + 1,)),
-            *Local.scratch(cells, late),
-        ],
+        out_specs=(hbm, vmem),
+        scratch_shapes=[pltpu.SemaphoreType.DMA, *Local.scratch(cells, late)],
         compiler_params=params,
         cost_estimate=pl.CostEstimate(flops=1 << 24, bytes_accessed=1 << 24, transcendentals=0),
         name="local_late",
     )(answers, table, rows, live, xyz, loc_early)
-    rem_values = jnp.sum(returned, axis=0)[0:5, 0:slots]
+    loc_values, rem_values = pl.pallas_call(
+        functools.partial(final_kernel, early),
+        out_shape=(
+            jax.ShapeDtypeStruct((5, loc), jnp.float32),
+            jax.ShapeDtypeStruct((5, slots), jnp.float32),
+        ),
+        in_specs=[anyw, vmem, vmem, hbm],
+        out_specs=(hbm, hbm),
+        scratch_shapes=[pltpu.VMEM((5, slots), jnp.float32), pltpu.SemaphoreType.DMA((2,))],
+        input_output_aliases={3: 0},
+        compiler_params=params,
+        name="final",
+    )(live, stage, returned, loc_part)
     return (loc_values, rem_values)
 
 

time: 30.2 us -> 27.8 us (0.921)
  Pallas kernels: 15 us -> 13.2 us
  other arithmetic: 0.6 us -> 0 us
    pallas_call x1, Pallas kernels: 6.05 us -> 4.45 us  [per_device(): pl.pallas_call(functools.partial(second_kernel, early, loc // GROUP, help...]
    pallas_call x1, Pallas kernels: 5.77 us -> 5.08 us  [per_device(): pl.pallas_call(functools.partial(first_kernel, early, help_count), out_sh...]
    pallas_call x0 -> x1, Pallas kernels: none -> 0.69 us  [per_device(): pl.pallas_call(functools.partial(final_kernel, early), out_shape=(jax.Sha...]
    reduce_sum x1 -> x0, other arithmetic: 0.6 us -> none  [per_device(): rem_values = jnp.sum(returned, axis=0)[0:5, 0:slots]]
  transfers between devices with their start and end apart: 2 -> 2, of which waited for: 0 -> 0; matrix products, arithmetic and copies ran while one was open for 0% -> 0% of each run, Pallas kernels for 40% -> 35%
where the time goes in v3:
time: 27.8 us; the launch traced here: 27.5 us
  Pallas kernels  13.2 us (47%)
  starting transfers between devices  12.9 us (46%)
  between operations  1.33 us (5%)
    all_to_all x1, starting transfers between devices, per_device(): asked = exchange(request)  7.83 us
    all_to_all x1, starting transfers between devices, per_device(): returned = exchange(answers)  5.11 us
    pallas_call x1, Pallas kernels, per_device(): pl.pallas_call(functools.partial(first_kernel, early, help_count), out_sh...  5.08 us
    pallas_call x1, Pallas kernels, per_device(): pl.pallas_call(functools.partial(second_kernel, early, loc // GROUP, help...  4.45 us
    pallas_call x1, Pallas kernels, per_device(): pl.pallas_call(answer_kernel, out_shape=jax.ShapeDtypeStruct((grid, 8, wi...  1.53 us
    pallas_call x1, Pallas kernels, per_device(): pl.pallas_call(functools.partial(request_kernel, lead), out_shape=jax.Sha...  1.47 us
    pallas_call x1, Pallas kernels, per_device(): pl.pallas_call(functools.partial(final_kernel, early), out_shape=(jax.Sha...  0.69 us
  transfers between devices with their start and end apart: 2, of which 0 were waited for; matrix products, arithmetic and copies ran while one was open for 0% of the time, Pallas kernels for 35%

profile of v3, /device:TPU:0, one launch (start us, length us, event | category | flops | bytes accessed | tf_op | source)
XLA Modules:
  0.0 27.5 jit_solution(8843371514754028474)
XLA Ops:
  0.6 1.5 %request.1._ = f32[8,4,128]{2,1,0:T(4,128)} custom-call(f32[3,32]{1,0:T(4,128)} %xyz_hbm.2, s32[1,32]{1,0:T(1,128)} %bitcast.3, s32[1,8]{1,0:T(1,128)} %count_hbm.1), custom_call_target="tpu_custom_call" | custom-call | tf_op jit(solution)/shard_map/request/pallas_call | solution.py:398
  2.1 7.8 %all-to-all-start = ((f32[8,4,128]{2,1,0:T(4,128)}), f32[8,4,128]{2,1,0:T(4,128)S(1)}, u32[]{:S(2)}, u32[]{:S(2)}) async-start(f32[8,4,128]{2,1,0:T(4,128)} %request.1._), calls=%async_computation | async-start | bytes 32768 | tf_op jit(solution)/shard_map/all_to_all | solution.py:412
  10.6 5.1 %local_early.1 = (f32[4096,128]{1,0:T(8,128)S(1)}, s32[64,128]{1,0:T(8,128)S(1)}, s32[8,128]{1,0:T(8,128)S(1)}, f32[3,8192]{1,0:T(4,128)S(1)}, f32[5,4096]{1,0:T(8,128)S(1)}) custom-call(f32[8,4,128]{2,1,0:T(4,128)} %request.1._, f32[24,8192]{1,0:T(8,128)} %corners_hbm.1, f32[40,8192]{1,0:T(8,128)} %solution_hbm.1, s32[64,128]{1,0:T(8,128)} %bitcast.2, ...), custom_call_target="tpu_custom_call" | custom-call | flops 16777216 | bytes 16777216 | tf_op jit(solution)/shard_map/local_early/pallas_call | solution.py:413
  15.7 0.0 all-to-all-done.request_ref
  15.7 1.5 %answer.1._ = f32[8,8,128]{2,1,0:T(8,128)} custom-call(f32[8,4,128]{2,1,0:T(4,128)S(1)} %all-to-all-done.request_ref, f32[4096,128]{1,0:T(8,128)S(1)} %get-tuple-element.10.table_ref.table), custom_call_target="tpu_custom_call" | custom-call | tf_op jit(solution)/shard_map/answer/pallas_call | solution.py:437
  17.2 5.1 %all-to-all-start.1 = ((f32[8,8,128]{2,1,0:T(8,128)}), f32[8,8,128]{2,1,0:T(8,128)S(1)}, u32[]{:S(2)}, u32[]{:S(2)}) async-start(f32[8,8,128]{2,1,0:T(8,128)} %answer.1._), calls=%async_computation.1 | async-start | bytes 65536 | tf_op jit(solution)/shard_map/all_to_all | solution.py:452
  22.3 4.5 %local_late.1 = (f32[5,8192]{1,0:T(8,128)}, f32[5,6144]{1,0:T(8,128)S(1)}) custom-call(f32[8,8,128]{2,1,0:T(8,128)} %answer.1._, f32[4096,128]{1,0:T(8,128)S(1)} %get-tuple-element.10.table_ref.table, s32[64,128]{1,0:T(8,128)S(1)} %get-tuple-element.11.rows, s32[8,128]{1,0:T(8,128)S(1)} %get-tuple-element.9.live._, f32[3,8192]{1,0:T(4,128)S(1)} %get-tuple-element.12.xyz, ...), custom_call_target="tpu_custom_call" | custom-call | flops 16777216 | bytes 16777216 | tf_op jit(solution)/shard_map/local_late/pallas_call | solution.py:454
  26.8 0.0 all-to-all-done.1.returned
  26.8 0.7 %final.1 = (f32[5,8192]{1,0:T(8,128)}, f32[5,32]{1,0:T(8,128)}) custom-call(s32[8,128]{1,0:T(8,128)S(1)} %get-tuple-element.9.live._, f32[5,6144]{1,0:T(8,128)S(1)} %get-tuple-element.14.stage, f32[8,8,128]{2,1,0:T(8,128)S(1)} %all-to-all-done.1.returned, f32[5,8192]{1,0:T(8,128)} %get-tuple-element.15.before_hbm), custom_call_target="tpu_custom_call", output_to_operand_aliasing={{0}: (3, {})} | custom-call | tf_op jit(solution)/shard_map/final/pallas_call | solution.py:467
Async XLA Ops:
  2.1 13.6 %all-to-all-start = ((f32[8,4,128]{2,1,0:T(4,128)}), f32[8,4,128]{2,1,0:T(4,128)S(1)}, u32[]{:S(2)}, u32[]{:S(2)}) async-start(f32[8,4,128]{2,1,0:T(4,128)} %request.1._), calls=%async_computation | async-start | bytes 32768 | tf_op jit(solution)/shard_map/all_to_all | solution.py:412
  17.2 9.6 %all-to-all-start.1 = ((f32[8,8,128]{2,1,0:T(8,128)}), f32[8,8,128]{2,1,0:T(8,128)S(1)}, u32[]{:S(2)}, u32[]{:S(2)}) async-start(f32[8,8,128]{2,1,0:T(8,128)} %answer.1._), calls=%async_computation.1 | async-start | bytes 65536 | tf_op jit(solution)/shard_map/all_to_all | solution.py:452

commit v4 on v3

--- a/solution.py
+++ b/solution.py
@@ -12,7 +12,7 @@
 ROWS = 64
 VMEM_BYTES = 32 << 20
 EARLY = 3
-LEAD = 3
+LEAD = 4
 WIDEN = 16
 QUARTERS = 4
 STRIDE = 72
@@ -326,14 +326,14 @@
     rem.wait()
 
 
-def answer_kernel(request_ref, table_ref, out_ref, rows, cells, cell_smem, buf, sem):
+def answer_kernel(request_ref, table_ref, out_ref, rows, buf):
     grid, depth, _ = request_ref.shape
     half = table_ref.shape[0]
     blocks = out_ref.shape[2] // LANES
     mine = lax.axis_index("grid")
     for c in range(depth):
         rows[pl.ds(c * grid, grid), :] = request_ref[:, c, :]
-    asked_all = []
+    asked_all, cells = [], []
     for k in range(blocks):
         count = min(LANES, grid * depth - k * LANES)
         asked = rows[k * LANES : k * LANES + count, :]
@@ -341,14 +341,11 @@
             asked = jnp.concatenate([asked, jnp.zeros((LANES - count, LANES), jnp.float32)], 0)
         asked_all.append(asked.T[ROWS : ROWS + 8, :])
         number = asked_all[k][3:4, :].astype(jnp.int32)
-        cells[k : k + 1, :] = jnp.where(number >= half, number - half, number)
-    copy = pltpu.make_async_copy(cells, cell_smem, sem)
-    copy.start()
-    copy.wait()
+        cells.append(jnp.where(number >= half, number - half, number))
     lane = lax.broadcasted_iota(jnp.int32, (8, LANES), 1)
     for k in range(blocks):
         for j in range(min(LANES, grid * depth - k * LANES)):
-            buf[j : j + 1, :] = table_ref[pl.ds(cell_smem[k, j], 1), :]
+            buf[j : j + 1, :] = table_ref[pl.ds(cells[k][0, j], 1), :]
         turned = buf[...].T
         asked = asked_all[k]
         upper = asked[3:4, :] >= float(half)
@@ -441,10 +438,7 @@
         out_specs=vmem,
         scratch_shapes=[
             pltpu.VMEM((slots, LANES), jnp.float32),
-            pltpu.VMEM((width // LANES, LANES), jnp.int32),
-            pltpu.SMEM((width // LANES, LANES), jnp.int32),
             pltpu.VMEM((LANES, LANES), jnp.float32),
-            pltpu.SemaphoreType.DMA,
         ],
         compiler_params=params,
         name="answer",

time: 27.8 us -> 27.4 us (0.986)
  Pallas kernels: 13.2 us -> 12.8 us
    pallas_call x1, Pallas kernels: 1.53 us -> 1.12 us  [per_device(): pl.pallas_call(answer_kernel, out_shape=jax.ShapeDtypeStruct((grid, 8, wi...]
where the time goes in v4:
time: 27.4 us; the launch traced here: 27.1 us
  starting transfers between devices  12.9 us (47%)
  Pallas kernels  12.8 us (47%)
  between operations  1.32 us (5%)
    all_to_all x1, starting transfers between devices, per_device(): asked = exchange(request)  7.83 us
    all_to_all x1, starting transfers between devices, per_device(): returned = exchange(answers)  5.1 us
    pallas_call x1, Pallas kernels, per_device(): pl.pallas_call(functools.partial(first_kernel, early, help_count), out_sh...  5.08 us
    pallas_call x1, Pallas kernels, per_device(): pl.pallas_call(functools.partial(second_kernel, early, loc // GROUP, help...  4.45 us
    pallas_call x1, Pallas kernels, per_device(): pl.pallas_call(functools.partial(request_kernel, lead), out_shape=jax.Sha...  1.47 us
    pallas_call x1, Pallas kernels, per_device(): pl.pallas_call(answer_kernel, out_shape=jax.ShapeDtypeStruct((grid, 8, wi...  1.12 us
    pallas_call x1, Pallas kernels, per_device(): pl.pallas_call(functools.partial(final_kernel, early), out_shape=(jax.Sha...  0.69 us
  transfers between devices with their start and end apart: 2, of which 0 were waited for; matrix products, arithmetic and copies ran while one was open for 0% of the time, Pallas kernels for 35%

profile of v4, /device:TPU:0, one launch (start us, length us, event | category | flops | bytes accessed | tf_op | source)
XLA Modules:
  0.0 27.1 jit_solution(11450680519461788886)
XLA Ops:
  0.6 1.5 %request.1._ = f32[8,4,128]{2,1,0:T(4,128)} custom-call(f32[3,32]{1,0:T(4,128)} %xyz_hbm.2, s32[1,32]{1,0:T(1,128)} %bitcast.3, s32[1,8]{1,0:T(1,128)} %count_hbm.1), custom_call_target="tpu_custom_call" | custom-call | tf_op jit(solution)/shard_map/request/pallas_call | solution.py:395
  2.1 7.8 %all-to-all-start = ((f32[8,4,128]{2,1,0:T(4,128)}), f32[8,4,128]{2,1,0:T(4,128)S(1)}, u32[]{:S(2)}, u32[]{:S(2)}) async-start(f32[8,4,128]{2,1,0:T(4,128)} %request.1._), calls=%async_computation | async-start | bytes 32768 | tf_op jit(solution)/shard_map/all_to_all | solution.py:409
  10.6 5.1 %local_early.1 = (f32[4096,128]{1,0:T(8,128)S(1)}, s32[64,128]{1,0:T(8,128)S(1)}, s32[8,128]{1,0:T(8,128)S(1)}, f32[3,8192]{1,0:T(4,128)S(1)}, f32[5,4096]{1,0:T(8,128)S(1)}) custom-call(f32[8,4,128]{2,1,0:T(4,128)} %request.1._, f32[24,8192]{1,0:T(8,128)} %corners_hbm.1, f32[40,8192]{1,0:T(8,128)} %solution_hbm.1, s32[64,128]{1,0:T(8,128)} %bitcast.2, ...), custom_call_target="tpu_custom_call" | custom-call | flops 16777216 | bytes 16777216 | tf_op jit(solution)/shard_map/local_early/pallas_call | solution.py:410
  15.7 0.0 all-to-all-done.request_ref
  15.7 1.1 %answer.1._ = f32[8,8,128]{2,1,0:T(8,128)} custom-call(f32[8,4,128]{2,1,0:T(4,128)S(1)} %all-to-all-done.request_ref, f32[4096,128]{1,0:T(8,128)S(1)} %get-tuple-element.10.table_ref.table), custom_call_target="tpu_custom_call" | custom-call | tf_op jit(solution)/shard_map/answer/pallas_call | solution.py:434
  16.8 5.1 %all-to-all-start.1 = ((f32[8,8,128]{2,1,0:T(8,128)}), f32[8,8,128]{2,1,0:T(8,128)S(1)}, u32[]{:S(2)}, u32[]{:S(2)}) async-start(f32[8,8,128]{2,1,0:T(8,128)} %answer.1._), calls=%async_computation.1 | async-start | bytes 65536 | tf_op jit(solution)/shard_map/all_to_all | solution.py:446
  21.9 4.5 %local_late.1 = (f32[5,8192]{1,0:T(8,128)}, f32[5,6144]{1,0:T(8,128)S(1)}) custom-call(f32[8,8,128]{2,1,0:T(8,128)} %answer.1._, f32[4096,128]{1,0:T(8,128)S(1)} %get-tuple-element.10.table_ref.table, s32[64,128]{1,0:T(8,128)S(1)} %get-tuple-element.11.rows, s32[8,128]{1,0:T(8,128)S(1)} %get-tuple-element.9.live._, f32[3,8192]{1,0:T(4,128)S(1)} %get-tuple-element.12.xyz, ...), custom_call_target="tpu_custom_call" | custom-call | flops 16777216 | bytes 16777216 | tf_op jit(solution)/shard_map/local_late/pallas_call | solution.py:448
  26.4 0.0 all-to-all-done.1.returned
  26.4 0.7 %final.1 = (f32[5,8192]{1,0:T(8,128)}, f32[5,32]{1,0:T(8,128)}) custom-call(s32[8,128]{1,0:T(8,128)S(1)} %get-tuple-element.9.live._, f32[5,6144]{1,0:T(8,128)S(1)} %get-tuple-element.14.stage, f32[8,8,128]{2,1,0:T(8,128)S(1)} %all-to-all-done.1.returned, f32[5,8192]{1,0:T(8,128)} %get-tuple-element.15.before_hbm), custom_call_target="tpu_custom_call", output_to_operand_aliasing={{0}: (3, {})} | custom-call | tf_op jit(solution)/shard_map/final/pallas_call | solution.py:461
Async XLA Ops:
  2.1 13.6 %all-to-all-start = ((f32[8,4,128]{2,1,0:T(4,128)}), f32[8,4,128]{2,1,0:T(4,128)S(1)}, u32[]{:S(2)}, u32[]{:S(2)}) async-start(f32[8,4,128]{2,1,0:T(4,128)} %request.1._), calls=%async_computation | async-start | bytes 32768 | tf_op jit(solution)/shard_map/all_to_all | solution.py:409
  16.8 9.6 %all-to-all-start.1 = ((f32[8,8,128]{2,1,0:T(8,128)}), f32[8,8,128]{2,1,0:T(8,128)S(1)}, u32[]{:S(2)}, u32[]{:S(2)}) async-start(f32[8,8,128]{2,1,0:T(8,128)} %answer.1._), calls=%async_computation.1 | async-start | bytes 65536 | tf_op jit(solution)/shard_map/all_to_all | solution.py:446

commit v5 on v4

--- a/solution.py
+++ b/solution.py
@@ -13,7 +13,7 @@
 VMEM_BYTES = 32 << 20
 EARLY = 3
 LEAD = 4
-WIDEN = 16
+WIDEN = 32
 QUARTERS = 4
 STRIDE = 72
 
@@ -164,6 +164,19 @@
             lanes = slice(h * ROWS, (h + 1) * ROWS)
             for j in range(LANES):
                 self.buf[k][j : j + 1, lanes] = self.wide[pl.ds(self.smem[k][h, j], 1), lanes]
+
+    def swap(self, table, lower=False):
+        half = table.shape[0]
+
+        def chunk(t, _):
+            at = pl.multiple_of(t * LANES, LANES)
+            both = table[pl.ds(at, LANES), :]
+            if lower:
+                self.wide[pl.ds(at, LANES), :] = both
+            self.wide[pl.ds(pl.multiple_of(half + at, LANES), LANES), :] = pltpu.roll(both, ROWS, 1)
+            return 0
+
+        lax.fori_loop(0, half // LANES, chunk, 0, unroll=WIDEN)
 
     def begin(self):
         for k in range(QUARTERS):
@@ -281,10 +294,10 @@
             ).T
             table[pl.ds(low, LANES), :] = both
             local.wide[pl.ds(low, LANES), :] = both
-            local.wide[pl.ds(high, LANES), :] = pltpu.roll(both, ROWS, 1)
             return 0
 
         lax.fori_loop(0, piece // LANES, chunk, 0, unroll=min(16, piece // LANES))
+    local.swap(table)
     for c in small[1:]:
         c.wait()
     live[...] = jnp.broadcast_to(live_one[...], live.shape)
@@ -298,16 +311,7 @@
     before.start()
     local = Local(first, last, help_count, rows, live, xyz, stage, lambda g: None, *scratch)
     local.begin()
-    half = table.shape[0]
-
-    def chunk(t, _):
-        at = pl.multiple_of(t * LANES, LANES)
-        both = table[pl.ds(at, LANES), :]
-        local.wide[pl.ds(at, LANES), :] = both
-        local.wide[pl.ds(pl.multiple_of(half + at, LANES), LANES), :] = pltpu.roll(both, ROWS, 1)
-        return 0
-
-    lax.fori_loop(0, half // LANES, chunk, 0, unroll=WIDEN)
+    local.swap(table, True)
     local.run()
     before.wait()
 

time: 27.4 us -> 27.2 us (level)
  no operation moved by 1% of the time
where the time goes in v5:
time: 27.2 us; the launch traced here: 26.9 us
  starting transfers between devices  12.9 us (47%)
  Pallas kernels  12.6 us (46%)
  between operations  1.32 us (5%)
    all_to_all x1, starting transfers between devices, per_device(): asked = exchange(request)  7.83 us
    all_to_all x1, starting transfers between devices, per_device(): returned = exchange(answers)  5.1 us
    pallas_call x1, Pallas kernels, per_device(): pl.pallas_call(functools.partial(first_kernel, early, help_count), out_sh...  4.98 us
    pallas_call x1, Pallas kernels, per_device(): pl.pallas_call(functools.partial(second_kernel, early, loc // GROUP, help...  4.37 us
    pallas_call x1, Pallas kernels, per_device(): pl.pallas_call(functools.partial(request_kernel, lead), out_shape=jax.Sha...  1.47 us
    pallas_call x1, Pallas kernels, per_device(): pl.pallas_call(answer_kernel, out_shape=jax.ShapeDtypeStruct((grid, 8, wi...  1.12 us
    pallas_call x1, Pallas kernels, per_device(): pl.pallas_call(functools.partial(final_kernel, early), out_shape=(jax.Sha...  0.69 us
  transfers between devices with their start and end apart: 2, of which 0 were waited for; matrix products, arithmetic and copies ran while one was open for 0% of the time, Pallas kernels for 35%

profile of v5, /device:TPU:0, one launch (start us, length us, event | category | flops | bytes accessed | tf_op | source)
XLA Modules:
  0.0 26.9 jit_solution(16912141929029075474)
XLA Ops:
  0.6 1.5 %request.1._ = f32[8,4,128]{2,1,0:T(4,128)} custom-call(f32[3,32]{1,0:T(4,128)} %xyz_hbm.2, s32[1,32]{1,0:T(1,128)} %bitcast.3, s32[1,8]{1,0:T(1,128)} %count_hbm.1), custom_call_target="tpu_custom_call" | custom-call | tf_op jit(solution)/shard_map/request/pallas_call | solution.py:399
  2.1 7.8 %all-to-all-start = ((f32[8,4,128]{2,1,0:T(4,128)}), f32[8,4,128]{2,1,0:T(4,128)S(1)}, u32[]{:S(2)}, u32[]{:S(2)}) async-start(f32[8,4,128]{2,1,0:T(4,128)} %request.1._), calls=%async_computation | async-start | bytes 32768 | tf_op jit(solution)/shard_map/all_to_all | solution.py:413
  10.6 5.0 %local_early.1 = (f32[4096,128]{1,0:T(8,128)S(1)}, s32[64,128]{1,0:T(8,128)S(1)}, s32[8,128]{1,0:T(8,128)S(1)}, f32[3,8192]{1,0:T(4,128)S(1)}, f32[5,4096]{1,0:T(8,128)S(1)}) custom-call(f32[8,4,128]{2,1,0:T(4,128)} %request.1._, f32[24,8192]{1,0:T(8,128)} %corners_hbm.1, f32[40,8192]{1,0:T(8,128)} %solution_hbm.1, s32[64,128]{1,0:T(8,128)} %bitcast.2, ...), custom_call_target="tpu_custom_call" | custom-call | flops 16777216 | bytes 16777216 | tf_op jit(solution)/shard_map/local_early/pallas_call | solution.py:414
  15.6 0.0 all-to-all-done.request_ref
  15.6 1.1 %answer.1._ = f32[8,8,128]{2,1,0:T(8,128)} custom-call(f32[8,4,128]{2,1,0:T(4,128)S(1)} %all-to-all-done.request_ref, f32[4096,128]{1,0:T(8,128)S(1)} %get-tuple-element.10.table_ref.table), custom_call_target="tpu_custom_call" | custom-call | tf_op jit(solution)/shard_map/answer/pallas_call | solution.py:438
  16.7 5.1 %all-to-all-start.1 = ((f32[8,8,128]{2,1,0:T(8,128)}), f32[8,8,128]{2,1,0:T(8,128)S(1)}, u32[]{:S(2)}, u32[]{:S(2)}) async-start(f32[8,8,128]{2,1,0:T(8,128)} %answer.1._), calls=%async_computation.1 | async-start | bytes 65536 | tf_op jit(solution)/shard_map/all_to_all | solution.py:450
  21.8 4.4 %local_late.1 = (f32[5,8192]{1,0:T(8,128)}, f32[5,6144]{1,0:T(8,128)S(1)}) custom-call(f32[8,8,128]{2,1,0:T(8,128)} %answer.1._, f32[4096,128]{1,0:T(8,128)S(1)} %get-tuple-element.10.table_ref.table, s32[64,128]{1,0:T(8,128)S(1)} %get-tuple-element.11.rows, s32[8,128]{1,0:T(8,128)S(1)} %get-tuple-element.9.live._, f32[3,8192]{1,0:T(4,128)S(1)} %get-tuple-element.12.xyz, ...), custom_call_target="tpu_custom_call" | custom-call | flops 16777216 | bytes 16777216 | tf_op jit(solution)/shard_map/local_late/pallas_call | solution.py:452
  26.2 0.0 all-to-all-done.1.returned
  26.2 0.7 %final.1 = (f32[5,8192]{1,0:T(8,128)}, f32[5,32]{1,0:T(8,128)}) custom-call(s32[8,128]{1,0:T(8,128)S(1)} %get-tuple-element.9.live._, f32[5,6144]{1,0:T(8,128)S(1)} %get-tuple-element.14.stage, f32[8,8,128]{2,1,0:T(8,128)S(1)} %all-to-all-done.1.returned, f32[5,8192]{1,0:T(8,128)} %get-tuple-element.15.before_hbm), custom_call_target="tpu_custom_call", output_to_operand_aliasing={{0}: (3, {})} | custom-call | tf_op jit(solution)/shard_map/final/pallas_call | solution.py:465
Async XLA Ops:
  2.1 13.5 %all-to-all-start = ((f32[8,4,128]{2,1,0:T(4,128)}), f32[8,4,128]{2,1,0:T(4,128)S(1)}, u32[]{:S(2)}, u32[]{:S(2)}) async-start(f32[8,4,128]{2,1,0:T(4,128)} %request.1._), calls=%async_computation | async-start | bytes 32768 | tf_op jit(solution)/shard_map/all_to_all | solution.py:413
  16.7 9.5 %all-to-all-start.1 = ((f32[8,8,128]{2,1,0:T(8,128)}), f32[8,8,128]{2,1,0:T(8,128)S(1)}, u32[]{:S(2)}, u32[]{:S(2)}) async-start(f32[8,8,128]{2,1,0:T(8,128)} %answer.1._), calls=%async_computation.1 | async-start | bytes 65536 | tf_op jit(solution)/shard_map/all_to_all | solution.py:450
